TPU v7x, 32 devices: a whole 2x2x4 slice. The times are simulated.
32 devices in a mesh: group: 2 (over core), dp: 8 (over z, x), mp: 2 (over y).
Axes of the slice: x: 2, y: 2, z: 4, core: 2. Of those that a mesh axis runs over, the one named last changes fastest.
Arguments:
- noise_seeds: int32 [16], P(('group', 'dp')), may hold values from 0 to 16777215
- timestep_ids: int32 [16], P(('group', 'dp')), may hold values from 0 to 999
- gen_up: bfloat16 [3072, 6144], P(('group', 'dp'), 'mp'), may hold values from -0.109375 to 0.109375
- gen_down: bfloat16 [6144, 3072], P('mp', ('group', 'dp')), may hold values from -0.08930431 to 0.08930431
- score_qkv: bfloat16 [2, 3, 3072, 3072], P('group', None, None, 'mp'), may hold values from -0.109375 to 0.109375
- score_out: bfloat16 [2, 3072, 3072], P('group', 'mp'), may hold values from -0.109375 to 0.109375
Outputs:
- latents: bfloat16 [16, 256, 3072], P(('group', 'dp'), None, 'mp')
- score_gap: bfloat16 [16, 256, 3072], P(('group', 'dp'), None, 'mp')
- grad_up: bfloat16 [3072, 6144], P(('group', 'dp'), 'mp')
- grad_down: bfloat16 [6144, 3072], P('mp', ('group', 'dp'))
All inputs are finite; a program needn't handle non-finite values.
Results may differ from a plain program's by a relative error of at most 0.03.
Values may be sent and summed in bfloat16 or wider, within the bound.
A program may use at most 192 MiB of HBM per device.

v0:
```python
import jax
import jax.numpy as jnp
from jax import lax
from jax.sharding import PartitionSpec as P

D = 3072
HEAD_DIM = 128
SEQ = 256
STEPS = 1000


NORM_EPS = 1e-06
ROOT_THREE = 1.7320508
GELU_SCALE = 0.7978845608


def partner_2(shard, axis, apart):
    return lax.ppermute(shard, axis, [(i, i ^ 1 << apart) for i in range(lax.axis_size(axis))])


def hashed(seed_grid, stream, feat_count, length):
    shape = (1, length, feat_count)
    tokens = lax.broadcasted_iota(jnp.int32, shape, 1)
    feature = lax.broadcasted_iota(jnp.int32, shape, 2)
    mixing = seed_grid * 747796405 + stream * 374761393 + tokens * 1103515245 + feature * 668265263
    mixing = mixing ^ mixing >> 15
    mixing = mixing * 1274126177
    mixing = mixing ^ mixing >> 13
    mixing = mixing * 1911520717
    mixing = mixing ^ mixing >> 16
    level = (mixing >> 7 & 65535).astype(jnp.float32)
    return ((level + 0.5) * (2.0 / 65536.0) - 1.0) * ROOT_THREE


def rms_norm(value):
    return value * lax.rsqrt(jnp.mean(value * value, axis=-1, keepdims=True) + NORM_EPS)


def gelu_slope(value):
    inner = GELU_SCALE * (value + 0.044715 * value * value * value)
    bend = jnp.tanh(inner)
    return 0.5 * (1.0 + bend) + 0.5 * value * (1.0 - bend * bend) * GELU_SCALE * (
        1.0 + 3.0 * 0.044715 * value * value
    )


def score_forward(paired, weights_in, weights_out):
    pairs = paired.shape[0]
    local_heads = weights_in.shape[2] // HEAD_DIM
    normed = rms_norm(paired.astype(jnp.float32)).astype(jnp.bfloat16)
    projected = jnp.einsum(
        "bsd,kdh->kbsh", normed, weights_in, preferred_element_type=jnp.float32
    ).astype(jnp.bfloat16)
    shape = (pairs, SEQ, local_heads, HEAD_DIM)
    query = projected[0].reshape(shape)
    keys = projected[1].reshape(shape)
    values = projected[2].reshape(shape)
    scores = jnp.einsum(
        "bqhe,bkhe->bhqk", query, keys, preferred_element_type=jnp.float32
    ) * HEAD_DIM ** (-0.5)
    expo = jnp.exp(scores)
    probs = (expo / jnp.sum(expo, axis=-1, keepdims=True)).astype(jnp.bfloat16)
    attended = jnp.einsum(
        "bhqk,bkhe->bqhe", probs, values, preferred_element_type=jnp.float32
    ).astype(jnp.bfloat16)
    attended = attended.reshape(pairs * SEQ, local_heads * HEAD_DIM)
    return jnp.dot(attended, weights_out, preferred_element_type=jnp.float32).reshape(
        pairs, SEQ, -1
    )


def difference(predicted, partner, own_group):
    own_pred = lax.dynamic_index_in_dim(predicted, own_group, 0, keepdims=False)
    flip_sign = (2 * own_group - 1).astype(jnp.float32)
    return (flip_sign * (own_pred.astype(jnp.float32) - partner.astype(jnp.float32))).astype(
        jnp.bfloat16
    )


def per_device(noise_seeds, timestep_ids, gen_up, gen_down, score_qkv, score_out):
    batch_size = lax.axis_size("group") * lax.axis_size("dp")
    width = D // lax.axis_size("mp")
    offset = lax.axis_index("mp") * width
    own_group = lax.axis_index("group")
    seed_grid = noise_seeds[:, None, None]
    start_noise = hashed(seed_grid, 0, D, SEQ)[0]
    normed = rms_norm(start_noise).astype(jnp.bfloat16)
    columns = normed
    before = jnp.dot(
        columns,
        lax.all_gather(gen_up, ("group", "dp"), axis=0, tiled=True),
        preferred_element_type=jnp.float32,
    )
    hidden = jax.nn.gelu(before, approximate=True).astype(jnp.bfloat16)
    partial_value = jnp.dot(
        hidden,
        lax.all_gather(gen_down, ("group", "dp"), axis=1, tiled=True),
        preferred_element_type=jnp.float32,
    )
    shift = (timestep_ids.astype(jnp.float32) + 0.5) / STEPS
    mixed = lax.psum(partial_value.astype(jnp.bfloat16), "mp").astype(jnp.float32)
    latent_full = (start_noise + mixed).astype(jnp.bfloat16)
    latent = lax.dynamic_slice_in_dim(latent_full, offset, width, 1)
    fresh = hashed(seed_grid, 1, D, SEQ)[0]
    noisy = ((1.0 - shift) * latent_full.astype(jnp.float32) + shift * fresh).astype(jnp.bfloat16)
    paired = lax.all_gather(noisy[None], "group", axis=0, tiled=True)
    partial_out = score_forward(paired, score_qkv[0], score_out[0])
    predicted = lax.psum(partial_out.astype(jnp.bfloat16), "mp")
    sent = lax.dynamic_index_in_dim(predicted, 1 - own_group, 0, keepdims=False)
    partner = partner_2(sent, "group", 0)
    gap_full = difference(predicted, partner, own_group)
    gap = lax.dynamic_slice_in_dim(gap_full, offset, width, 1)
    down_local = (
        lax.dot_general(
            hidden, gap_full, (((0,), (0,)), ((), ())), preferred_element_type=jnp.float32
        )
        / batch_size
    )
    grad_down = lax.psum_scatter(
        down_local.astype(jnp.bfloat16), ("group", "dp"), scatter_dimension=1, tiled=True
    )
    columns = gap_full
    slope = lax.dot_general(
        columns,
        lax.all_gather(gen_down, ("group", "dp"), axis=1, tiled=True),
        (((1,), (1,)), ((), ())),
        preferred_element_type=jnp.float32,
    )
    change = (slope * gelu_slope(before)).astype(jnp.bfloat16)
    grad_up = lax.psum_scatter(
        (
            lax.dot_general(
                normed, change, (((0,), (0,)), ((), ())), preferred_element_type=jnp.float32
            )
            / batch_size
        ).astype(jnp.bfloat16),
        ("group", "dp"),
        scatter_dimension=0,
        tiled=True,
    )
    return (latent[None], gap[None], grad_up, grad_down)


def solution(mesh):
    in_specs = (
        P(("group", "dp")),
        P(("group", "dp")),
        P(("group", "dp"), "mp"),
        P("mp", ("group", "dp")),
        P("group", None, None, "mp"),
        P("group", "mp", None),
    )
    out_specs = (
        P(("group", "dp"), None, "mp"),
        P(("group", "dp"), None, "mp"),
        P(("group", "dp"), "mp"),
        P("mp", ("group", "dp")),
    )
    return jax.shard_map(
        per_device, mesh=mesh, in_specs=in_specs, out_specs=out_specs, check_vma=False
    )
```

profile of v0, /device:TPU:0, one launch (start us, length us, event | category | flops | bytes accessed | tf_op | source)
XLA Modules:
  0.0 847.7 jit_solution(9924228217682029638)
XLA Ops:
  7.2 0.0 all-gather.5.cloned.1.call-start
  7.2 0.7 all-gather.5.cloned.1.call-update
  7.9 0.0 all-gather.7.cloned.1.call-start
  7.9 0.7 all-gather.7.cloned.1.call-update
  8.6 0.0 all-reduce.3.cloned.1.call-start
  9.4 2.0 multiply_reduce_fusion
  11.3 99.9 %all-gather.5.cloned.1.call-done = bf16[3072,3072]{1,0:T(8,128)(2,1)} async-done(((bf16[192,3072]{1,0:T(8,128)(2,1)}), bf16[3072,3072]{1,0:T(8,128)(2,1)}) %all-gather.5.cloned.1.call-update) | async-done | bytes 18874384 | tf_op jit(solution)/shard_map/all_gather | solution.py:91
  111.3 10.7 %fusion.52 = f32[256,3072]{1,0:T(8,128)S(1)} fusion(bf16[3072,3072]{1,0:T(8,128)(2,1)} %all-gather.5.cloned.1.call-done, f32[256]{0:T(256)S(1)} %rsqrt_multiply_fusion, s32[3072]{0:T(1024)S(1)} %iota_multiply_fusion, s32[256]{0:T(256)S(1)} %fusion.54), kind=kOutput, calls=%fused_computation.70 | convolution fusion | flops 4845207552 | bytes 22034432 | tf_op jit(solution)/shard_map/dot_general | solution.py:89
  122.0 0.0 copy-start.3
  122.0 89.8 %all-gather.7.cloned.1.call-done = bf16[3072,3072]{0,1:T(8,128)(2,1)} async-done(((bf16[3072,192]{0,1:T(8,128)(2,1)}), bf16[3072,3072]{0,1:T(8,128)(2,1)}) %all-gather.7.cloned.1.call-update) | async-done | bytes 18874384 | tf_op jit(solution)/shard_map/all_gather | solution.py:97
  211.9 10.5 %convolution_convert_fusion = bf16[256,3072]{1,0:T(8,128)(2,1)} fusion(bf16[3072,3072]{0,1:T(8,128)(2,1)} %all-gather.7.cloned.1.call-done, f32[256,3072]{1,0:T(8,128)S(1)} %fusion.52), kind=kOutput, calls=%fused_computation.25 | convolution fusion | flops 4839702528 | bytes 23592960 | tf_op jit(solution)/shard_map/dot_general | solution.py:95
  222.4 0.0 copy-done.3
  222.4 0.0 all-reduce.3.cloned.1.call-update
  222.4 0.0 all-gather.9.cloned.1.call-start
  223.1 50.9 %all-reduce.3.cloned.1.call-done = bf16[256,3072]{1,0:T(8,128)(2,1)} async-done(((bf16[256,3072]{1,0:T(8,128)(2,1)}), bf16[256,3072]{1,0:T(8,128)(2,1)}) %all-reduce.3.cloned.1.call-update) | async-done | bytes 1572880 | tf_op jit(solution)/shard_map/psum | solution.py:101
  274.1 6.3 fusion.49
  280.3 0.0 all-gather.9.cloned.1.call-update
  280.3 0.2 all-reduce.5.cloned.1.call-start
  280.6 12.0 %all-gather.9.cloned.1.call-done = bf16[512,3072]{1,0:T(8,128)(2,1)} async-done(((bf16[256,3072]{1,0:T(8,128)(2,1)}), bf16[512,3072]{1,0:T(8,128)(2,1)}) %all-gather.9.cloned.1.call-update) | async-done | bytes 3145744 | tf_op jit(solution)/shard_map/all_gather | solution.py:106
  292.6 0.0 copy-start.1
  292.6 2.7 fusion.4
  295.4 0.1 copy-done.1
  295.4 19.0 %convert_bitcast_fusion = bf16[3,2,256,1536]{3,2,0,1:T(8,128)(2,1)S(1)} fusion(bf16[1,3,3072,1536]{3,2,1,0:T(8,128)(2,1)} %param.10, bf16[2,256,3072]{2,1,0:T(8,128)(2,1)S(1)} %bitcast.56, f32[2,256]{1,0:T(2,128)S(1)} %add_rsqrt_fusion), kind=kOutput, calls=%fused_computation.22 | convolution fusion | flops 14502592512 | bytes 36177920 | tf_op jit(solution)/shard_map/bsd,kdh->kbsh/dot_general | solution.py:51
  314.5 1.5 fusion.78
  316.0 1.6 copy.26
  317.5 1.7 copy.27
  319.2 1.6 copy.28
  320.9 0.0 copy-start.2
  320.9 0.0 slice-start
  320.9 2.9 fusion.6
  323.7 0.0 copy-done.2
  323.8 0.0 slice-start.1
  323.8 0.0 slice-start.2
  323.8 1.3 fusion.51
  325.1 0.0 slice-done
  325.1 0.9 slice-done.1
  326.0 0.2 slice-done.2
  326.2 6.6 fusion.9
  332.8 0.0 all-reduce.5.cloned.1.call-update
  332.8 0.3 reduce-scatter.5.cloned.1.call-start
  333.1 86.8 %all-reduce.5.cloned.1.call-done = bf16[2,256,3072]{2,1,0:T(8,128)(2,1)} async-done(((bf16[2,256,3072]{2,1,0:T(8,128)(2,1)}), bf16[2,256,3072]{2,1,0:T(8,128)(2,1)}) %all-reduce.5.cloned.1.call-update) | async-done | bytes 3145744 | tf_op jit(solution)/shard_map/psum | solution.py:108
  419.9 1.5 dynamic-slice_bitcast_fusion
  421.4 0.1 collective-permute-start
  421.5 0.0 copy-start.4
  421.5 3.4 collective-permute-done
  424.9 2.0 fusion.47
  426.9 0.0 copy-done.4
  426.9 9.9 %fusion.12 = bf16[256,3072]{1,0:T(8,128)(2,1)S(1)} fusion(bf16[256,3072]{1,0:T(8,128)(2,1)S(1)} %fusion.47, bf16[3072,3072]{0,1:T(8,128)(2,1)} %all-gather.7.cloned.1.call-done, f32[256,3072]{1,0:T(8,128)S(1)} %copy-done.4), kind=kOutput, calls=%fused_computation.26 | convolution fusion | flops 4846780416 | bytes 25165824 | tf_op jit(solution)/shard_map/dot_general | solution.py:123
  436.9 10.4 %multiply_convert_fusion.1 = bf16[3072,3072]{1,0:T(8,128)(2,1)} fusion(bf16[256,3072]{1,0:T(8,128)(2,1)S(1)} %fusion.12, f32[256]{0:T(256)S(1)} %rsqrt_multiply_fusion, s32[3072]{0:T(1024)S(1)} %iota_multiply_fusion, s32[256]{0:T(256)S(1)} %fusion.54), kind=kOutput, calls=%fused_computation.1 | convolution fusion | flops 4864081920 | bytes 20461568 | tf_op jit(solution)/shard_map/dot_general | solution.py:132
  447.2 0.0 reduce-scatter.5.cloned.1.call-update
  447.3 0.0 reduce-scatter.7.cloned.1.call-start
  447.3 14.8 %multiply_convert_fusion = bf16[3072,3072]{1,0:T(8,128)(2,1)} fusion(bf16[256,3072]{1,0:T(8,128)(2,1)S(1)} %fusion.47, f32[256,3072]{1,0:T(8,128)} %copy-done.3), kind=kOutput, calls=%fused_computation | convolution fusion | flops 4857790464 | bytes 23592960 | tf_op jit(solution)/shard_map/dot_general | solution.py:114
  462.2 25.8 %copy.41 = bf16[3072,3072]{0,1:T(8,128)(2,1)} copy(bf16[3072,3072]{1,0:T(8,128)(2,1)} %multiply_convert_fusion) | data formatting | bytes 37748736
  488.0 0.0 copy-start
  488.0 0.0 reduce-scatter.7.cloned.1.call-update
  488.0 1.4 copy-done
  489.4 0.9 dynamic-slice_bitcast_fusion.2
  490.3 0.9 dynamic-slice_bitcast_fusion.1
  491.2 151.0 %reduce-scatter.5.cloned.1.call-done = bf16[192,3072]{1,0:T(8,128)(2,1)} async-done(((bf16[3072,3072]{1,0:T(8,128)(2,1)}), bf16[192,3072]{1,0:T(8,128)(2,1)}) %reduce-scatter.5.cloned.1.call-update) | async-done | bytes 1179664 | tf_op jit(solution)/shard_map/reduce_scatter | solution.py:130
  642.2 198.6 %reduce-scatter.7.cloned.1.call-done = bf16[192,3072]{1,0:T(8,128)(2,1)} async-done(((bf16[3072,3072]{1,0:T(8,128)(2,1)}), bf16[192,3072]{1,0:T(8,128)(2,1)}) %reduce-scatter.7.cloned.1.call-update) | async-done | bytes 1179664
  (6 shorter events, 0.0 us)
Async XLA Ops:
  7.2 104.1 %all-gather.5.cloned.1.call-start = ((), (), s32[]{:S(2)}) async-start(), calls=%async_computation.2 | async-start | bytes 20054016 | tf_op jit(solution)/shard_map/all_gather | solution.py:91
  7.9 204.0 %all-gather.7.cloned.1.call-start = ((), (), s32[]{:S(2)}) async-start(), calls=%async_computation.3 | async-start | bytes 20054016 | tf_op jit(solution)/shard_map/all_gather | solution.py:97
  8.6 265.4 %all-reduce.3.cloned.1.call-start = ((), (), s32[]{:S(2)}) async-start(), calls=%async_computation.4 | async-start | bytes 3145728 | tf_op jit(solution)/shard_map/psum | solution.py:101
  122.0 100.3 %copy-start.3 = (f32[256,3072]{1,0:T(8,128)}, f32[256,3072]{1,0:T(8,128)S(1)}, u32[]{:S(2)}) copy-start(f32[256,3072]{1,0:T(8,128)S(1)} %fusion.52) | copy-start | bytes 9437188
  222.4 70.2 %all-gather.9.cloned.1.call-start = ((), (), s32[]{:S(2)}) async-start(), calls=%async_computation.7 | async-start | bytes 4718592 | tf_op jit(solution)/shard_map/all_gather | solution.py:106
  280.3 139.6 %all-reduce.5.cloned.1.call-start = ((), (), s32[]{:S(2)}) async-start(), calls=%async_computation.5 | async-start | bytes 6291456 | tf_op jit(solution)/shard_map/psum | solution.py:108
  292.6 2.8 copy-start.1
  320.9 2.9 copy-start.2
  320.9 4.3 slice-start
  323.8 2.3 slice-start.1
  323.8 2.5 slice-start.2
  332.8 309.4 %reduce-scatter.5.cloned.1.call-start = ((), (), s32[]{:S(2)}) async-start(), calls=%async_computation.6 | async-start | bytes 20054016 | tf_op jit(solution)/shard_map/reduce_scatter | solution.py:130
  421.4 3.5 collective-permute-start
  421.5 5.4 copy-start.4
  447.3 393.6 %reduce-scatter.7.cloned.1.call-start = ((), (), s32[]{:S(2)}) async-start(), calls=%async_computation.8 | async-start | bytes 20054016
  488.0 1.4 copy-start
Sparse Core Ops, SparseCore 0:
  9.6 101.6 all-gather.4
  112.9 98.9 all-gather.6
  222.5 51.4 all-reduce.2
  280.5 12.1 all-gather.8
  332.9 86.9 all-reduce.4
  447.4 194.7 reduce-scatter.4
  646.9 193.8 reduce-scatter.6
where the time goes:
time: 849 us; the launch traced here: 848 us
  waiting for transfers between devices  694 us (82%)
  matrix products  86.2 us (10%)
  local copies, waits for them, and re-layouts  38.1 us (4%)
  between operations  15.6 us (2%)
  other arithmetic  13 us (2%)
    unnamed x8, waiting for transfers between devices  200 us
    reduce_scatter x1, waiting for transfers between devices, per_device(): lax.psum_scatter((lax.dot_general(normed, change, (((0,), (0,)), ((), ())...  151 us
    all_gather x1, waiting for transfers between devices, per_device(): lax.all_gather(gen_up, ('group', 'dp'), axis=0, tiled=True)  99.9 us
    all_gather x1, waiting for transfers between devices, per_device(): lax.all_gather(gen_down, ('group', 'dp'), axis=1, tiled=True)  89.8 us
    psum x1, waiting for transfers between devices, per_device(): predicted = lax.psum(partial_out.astype(jnp.bfloat16), 'mp')  86.8 us
    psum x1, waiting for transfers between devices, per_device(): lax.psum(partial_value.astype(jnp.bfloat16), 'mp').astype(jnp.float32)  50.9 us
    unnamed x17, local copies, waits for them, and re-layouts  28.4 us
    dot_general x1, matrix products, score_forward(): jnp.einsum('bsd,kdh->kbsh', normed, weights_in, preferred_element_type=jn...  19 us
  transfers between devices with their start and end apart: 8, of which 8 were waited for; matrix products, arithmetic and copies ran while one was open for 7% of the time, Pallas kernels for 0%

commit v1 on v0

v1 whole, which is shorter than its diff:
```python
import jax
import jax.numpy as jnp
from jax import lax
from jax.sharding import PartitionSpec as P

D = 3072
HEAD_DIM = 128
SEQ = 256
STEPS = 1000


NORM_EPS = 1e-06
ROOT_THREE = 1.7320508
GELU_SCALE = 0.7978845608


def swap(shard, axis, bit):
    return lax.ppermute(shard, axis, [(i, i ^ bit) for i in range(lax.axis_size(axis))])


def bits_of(axis):
    return [1 << k for k in range(lax.axis_size(axis).bit_length() - 1)]


def xor_gather(shard, axis, order):
    bits = bits_of(axis)
    out = shard.reshape((1,) * len(bits) + shard.shape)
    for bit in order:
        out = jnp.concatenate([out, swap(out, axis, bit)], axis=bits.index(bit))
    return out


def xor_scatter(parts, axis, order):
    bits = bits_of(axis)
    for bit in order:
        at = bits.index(bit)
        kept = lax.slice_in_dim(parts, 0, 1, axis=at)
        sent = lax.slice_in_dim(parts, 1, 2, axis=at).astype(jnp.bfloat16)
        parts = kept.astype(jnp.float32) + swap(sent, axis, bit).astype(jnp.float32)
    return parts.reshape(parts.shape[len(bits):])


def tokens_to_features(shard, axis):
    count = lax.axis_size(axis)
    me = lax.axis_index(axis)
    tokens, width = shard.shape[0], shard.shape[1] // count
    out = jnp.zeros((count * tokens, width), shard.dtype)
    for mask in range(count):
        other = me ^ mask
        block = lax.dynamic_slice_in_dim(shard, other * width, width, 1)
        if mask:
            block = swap(block, axis, mask)
        out = lax.dynamic_update_slice_in_dim(out, block, other * tokens, 0)
    return out


def hashed(seed_grid, stream, tokens, feature):
    mixing = seed_grid * 747796405 + stream * 374761393 + tokens * 1103515245 + feature * 668265263
    mixing = mixing ^ mixing >> 15
    mixing = mixing * 1274126177
    mixing = mixing ^ mixing >> 13
    mixing = mixing * 1911520717
    mixing = mixing ^ mixing >> 16
    level = (mixing >> 7 & 65535).astype(jnp.float32)
    return ((level + 0.5) * (2.0 / 65536.0) - 1.0) * ROOT_THREE


def rms_norm(value):
    return value * lax.rsqrt(jnp.mean(value * value, axis=-1, keepdims=True) + NORM_EPS)


def gelu_slope(value):
    inner = GELU_SCALE * (value + 0.044715 * value * value * value)
    bend = jnp.tanh(inner)
    return 0.5 * (1.0 + bend) + 0.5 * value * (1.0 - bend * bend) * GELU_SCALE * (
        1.0 + 3.0 * 0.044715 * value * value
    )


def score_forward(normed, weights_in, weights_out):
    pairs, length = normed.shape[:2]
    local_heads = weights_in.shape[2] // HEAD_DIM
    projected = jnp.einsum(
        "bsd,kdh->kbsh", normed, weights_in, preferred_element_type=jnp.float32
    ).astype(jnp.bfloat16)
    shape = (pairs, length, local_heads, HEAD_DIM)
    query = projected[0].reshape(shape)
    keys = projected[1].reshape(shape)
    values = projected[2].reshape(shape)
    scores = jnp.einsum(
        "bqhe,bkhe->bhqk", query, keys, preferred_element_type=jnp.float32
    ) * HEAD_DIM ** (-0.5)
    expo = jnp.exp(scores)
    probs = (expo / jnp.sum(expo, axis=-1, keepdims=True)).astype(jnp.bfloat16)
    attended = jnp.einsum(
        "bhqk,bkhe->bqhe", probs, values, preferred_element_type=jnp.float32
    ).astype(jnp.bfloat16)
    attended = attended.reshape(pairs, length, local_heads * HEAD_DIM)
    return [
        jnp.dot(attended[pair], weights_out, preferred_element_type=jnp.float32)
        for pair in (1, 0)
    ]


def contract_first(left, right):
    return lax.dot_general(left, right, (((0,), (0,)), ((), ())), preferred_element_type=jnp.float32)


def per_device(noise_seeds, timestep_ids, gen_up, gen_down, score_qkv, score_out):
    n_dp, n_mp = lax.axis_size("dp"), lax.axis_size("mp")
    batch_size = lax.axis_size("group") * n_dp
    group, mp = lax.axis_index("group"), lax.axis_index("mp")
    dp_bits, mp_bits = bits_of("dp"), bits_of("mp")
    near_first = dp_bits
    far_first = dp_bits[1:] + dp_bits[:1]
    length = SEQ // n_mp
    half = D // 2

    up = lax.all_to_all(gen_up, "dp", split_axis=1, concat_axis=0, tiled=True)
    down = lax.all_to_all(gen_down, "dp", split_axis=0, concat_axis=1, tiled=True)
    share = up.shape[1]
    up = xor_gather(up, "mp", mp_bits).reshape(n_mp, half, share)
    up = up.transpose(1, 0, 2).reshape(half, n_mp * share)
    up = jnp.concatenate([up, swap(up, "group", 1)], axis=0)
    down = xor_gather(down, "mp", mp_bits).reshape(n_mp * share, half)
    down_other = swap(down, "group", 1)
    down = jnp.where(
        group == 0,
        jnp.concatenate([down, down_other], axis=1),
        jnp.concatenate([down_other, down], axis=1),
    )

    seeds = xor_gather(noise_seeds, "dp", near_first).reshape(n_dp, 1, 1)
    shape = (n_dp, length, D)
    tokens = lax.broadcasted_iota(jnp.int32, shape, 1) + mp * length
    feature = (lax.broadcasted_iota(jnp.int32, shape, 2) + group * half) % D
    normed = rms_norm(hashed(seeds, 0, tokens, feature)).astype(jnp.bfloat16)
    normed = normed.reshape(n_dp * length, D)
    before = jnp.dot(normed, up, preferred_element_type=jnp.float32)
    hidden = jax.nn.gelu(before, approximate=True).astype(jnp.bfloat16)

    def stacked(value):
        return value.reshape((2,) * len(dp_bits) + (length, value.shape[-1]))

    cut = D * 2 // 3
    near = jnp.dot(hidden, down[:, :cut], preferred_element_type=jnp.float32).astype(jnp.bfloat16)
    far = jnp.dot(hidden, down[:, cut:], preferred_element_type=jnp.float32).astype(jnp.bfloat16)
    mixed = jnp.concatenate(
        [
            xor_scatter(stacked(near), "dp", near_first),
            xor_scatter(stacked(far), "dp", far_first),
        ],
        axis=-1,
    )

    own_seed = noise_seeds[:, None]
    tokens = lax.broadcasted_iota(jnp.int32, (length, D), 0) + mp * length
    feature = lax.broadcasted_iota(jnp.int32, (length, D), 1)
    latent = (hashed(own_seed, 0, tokens, feature) + mixed).astype(jnp.bfloat16)
    shift = (timestep_ids.astype(jnp.float32) + 0.5) / STEPS
    fresh = hashed(own_seed, 1, tokens, feature)
    noisy = ((1.0 - shift) * latent.astype(jnp.float32) + shift * fresh).astype(jnp.bfloat16)
    score_normed = rms_norm(noisy.astype(jnp.float32)).astype(jnp.bfloat16)

    sample = xor_gather(score_normed, "mp", mp_bits).reshape(SEQ, D)
    paired = jnp.stack([sample, swap(sample, "group", 1)])
    latents = tokens_to_features(latent, "mp")
    other_pred, own_pred = score_forward(paired, score_qkv[0], score_out[0])
    partner = swap(other_pred.astype(jnp.bfloat16), "group", 1)
    flip_sign = (2 * group - 1).astype(jnp.float32)
    gap = flip_sign * (own_pred - partner.astype(jnp.float32))
    gap = xor_scatter(gap.reshape((2,) * len(mp_bits) + (length, D)), "mp", mp_bits)
    gap = gap.astype(jnp.bfloat16)
    gap_all = jnp.concatenate(
        [
            xor_gather(gap[:, :cut], "dp", near_first[::-1]).reshape(n_dp * length, cut),
            xor_gather(gap[:, cut:], "dp", far_first[::-1]).reshape(n_dp * length, D - cut),
        ],
        axis=1,
    )
    score_gap = tokens_to_features(gap, "mp")

    def over_batch(value):
        return value / batch_size

    down_sent = over_batch(
        contract_first(hidden, lax.dynamic_slice_in_dim(gap_all, (1 - group) * half, half, 1))
    ).astype(jnp.bfloat16)
    down_sent = swap(down_sent, "group", 1)
    down_kept = over_batch(
        contract_first(hidden, lax.dynamic_slice_in_dim(gap_all, group * half, half, 1))
    )
    grad_down = (down_kept + down_sent.astype(jnp.float32)).astype(jnp.bfloat16)
    grad_down = grad_down.reshape((2,) * len(mp_bits) + (share, half))
    grad_down = xor_scatter(grad_down, "mp", mp_bits).astype(jnp.bfloat16)
    grad_down = lax.all_to_all(grad_down, "dp", split_axis=1, concat_axis=0, tiled=True)

    slope = lax.dot_general(
        gap_all, down, (((1,), (1,)), ((), ())), preferred_element_type=jnp.float32
    )
    change = (slope * gelu_slope(before)).astype(jnp.bfloat16)
    up_sent = over_batch(contract_first(normed[:, half:], change)).astype(jnp.bfloat16)
    up_sent = swap(up_sent, "group", 1)
    up_kept = over_batch(contract_first(normed[:, :half], change))
    grad_up = (up_kept + up_sent.astype(jnp.float32)).astype(jnp.bfloat16)
    grad_up = jnp.moveaxis(grad_up.reshape(half, n_mp, share), 1, 0)
    grad_up = grad_up.reshape((2,) * len(mp_bits) + (half, share))
    grad_up = xor_scatter(grad_up, "mp", mp_bits).astype(jnp.bfloat16)
    grad_up = lax.all_to_all(grad_up, "dp", split_axis=0, concat_axis=1, tiled=True)
    return (latents[None], score_gap[None], grad_up, grad_down)


def solution(mesh):
    in_specs = (
        P(("group", "dp")),
        P(("group", "dp")),
        P(("group", "dp"), "mp"),
        P("mp", ("group", "dp")),
        P("group", None, None, "mp"),
        P("group", "mp", None),
    )
    out_specs = (
        P(("group", "dp"), None, "mp"),
        P(("group", "dp"), None, "mp"),
        P(("group", "dp"), "mp"),
        P("mp", ("group", "dp")),
    )
    return jax.shard_map(
        per_device, mesh=mesh, in_specs=in_specs, out_specs=out_specs, check_vma=False
    )
```

time: 849 us -> 578 us (0.68)
  waiting for transfers between devices: 694 us -> 363 us
  starting transfers between devices: 0.75 us -> 48.5 us
  other arithmetic: 13 us -> 41.4 us
  between operations: 15.6 us -> 3.13 us
    ppermute x1 -> x29, waiting for transfers between devices: 3.38 us -> 305 us  [swap(): lax.ppermute(shard, axis, [(i, i ^ bit) for i in range(lax.axis_size(axis...]
    all_gather x3 -> x0, waiting for transfers between devices: 202 us -> none  [the longest x1 99.9 us: per_device(): lax.all_gather(gen_up, ('group', 'dp'), axis=0, tiled=True)]
    unnamed x8 -> x0, waiting for transfers between devices: 200 us -> none
    reduce_scatter x1 -> x0, waiting for transfers between devices: 151 us -> none  [per_device(): lax.psum_scatter((lax.dot_general(normed, change, (((0,), (0,)), ((), ())...]
    psum x2 -> x0, waiting for transfers between devices: 138 us -> none  [the longest x1 86.8 us: per_device(): predicted = lax.psum(partial_out.astype(jnp.bfloat16), 'mp')]
    all_to_all x0 -> x4, waiting for transfers between devices: none -> 58.1 us  [the longest x1 27.4 us: per_device(): lax.all_to_all(gen_down, 'dp', split_axis=0, concat_axis=1, tiled=True)]
    ppermute x1 -> x29, starting transfers between devices: 0.07 us -> 27.7 us  [swap(): lax.ppermute(shard, axis, [(i, i ^ bit) for i in range(lax.axis_size(axis...]
    unnamed x17 -> x44, local copies, waits for them, and re-layouts: 28.4 us -> 1.05 us
  transfers between devices with their start and end apart: 8 -> 33, of which waited for: 8 -> 23; matrix products, arithmetic and copies ran while one was open for 7% -> 13% of each run, Pallas kernels for 0% -> 0%
where the time goes in v1:
time: 578 us; the launch traced here: 573 us
  waiting for transfers between devices  363 us (63%)
  matrix products  82 us (14%)
  starting transfers between devices  48.5 us (8%)
  other arithmetic  41.4 us (7%)
  local copies, waits for them, and re-layouts  34.8 us (6%)
    ppermute x29, waiting for transfers between devices, swap(): lax.ppermute(shard, axis, [(i, i ^ bit) for i in range(lax.axis_size(axis...  305 us
    ppermute x29, starting transfers between devices, swap(): lax.ppermute(shard, axis, [(i, i ^ bit) for i in range(lax.axis_size(axis...  27.7 us
    all_to_all x1, waiting for transfers between devices, per_device(): lax.all_to_all(gen_down, 'dp', split_axis=0, concat_axis=1, tiled=True)  27.4 us
    all_to_all x1, waiting for transfers between devices, per_device(): up = lax.all_to_all(gen_up, 'dp', split_axis=1, concat_axis=0, tiled=True)  23.9 us
    dot_general x4, matrix products, contract_first(): lax.dot_general(left, right, (((0,), (0,)), ((), ())), preferred_element_...  22.9 us
    dot_general x1, matrix products, score_forward(): jnp.einsum('bsd,kdh->kbsh', normed, weights_in, preferred_element_type=jn...  18.9 us
    dot_general x1, matrix products, per_device(): before = jnp.dot(normed, up, preferred_element_type=jnp.float32)  12.5 us
  transfers between devices with their start and end apart: 33, of which 23 were waited for; matrix products, arithmetic and copies ran while one was open for 13% of the time, Pallas kernels for 0%

profile of v1, /device:TPU:0, one launch (start us, length us, event | category | flops | bytes accessed | tf_op | source)
XLA Modules:
  0.0 573.0 jit_solution(12700090908436901973)
XLA Ops:
  0.6 2.5 copy.83
  3.1 7.3 %all-to-all-start.1 = ((bf16[8,384,192]{1,2,0:T(8,128)(2,1)}), bf16[8,384,192]{1,2,0:T(8,128)(2,1)S(1)}, u32[]{:S(2)}, u32[]{:S(2)}) async-start(bf16[8,384,192]{1,2,0:T(8,128)(2,1)} %bitcast.123), calls=%async_computation.1 | async-start | bytes 2359296 | tf_op jit(solution)/shard_map/all_to_all | solution.py:120
  11.6 27.4 %all-to-all-done.1 = bf16[8,384,192]{1,2,0:T(8,128)(2,1)S(1)} async-done(((bf16[8,384,192]{1,2,0:T(8,128)(2,1)}), bf16[8,384,192]{1,2,0:T(8,128)(2,1)S(1)}, u32[]{:S(2)}, u32[]{:S(2)}) %all-to-all-start.1) | async-done | bytes 1179680 | tf_op jit(solution)/shard_map/all_to_all | solution.py:120
  39.0 3.6 all-to-all-start
  42.6 1.5 collective-permute-start.5
  44.2 2.0 collective-permute-start
  47.5 23.9 %all-to-all-done = bf16[192,8,384]{2,0,1:T(8,128)(2,1)S(1)} async-done(((bf16[192,8,384]{2,0,1:T(8,128)(2,1)}), bf16[192,8,384]{2,0,1:T(8,128)(2,1)S(1)}, u32[]{:S(2)}, u32[]{:S(2)}) %all-to-all-start) | async-done | bytes 1179680 | tf_op jit(solution)/shard_map/all_to_all | solution.py:119
  74.8 3.6 collective-permute-done.1
  79.4 4.3 collective-permute-done.2
  85.1 1.9 pad_maximum_fusion.3
  87.0 2.6 copy.60
  90.3 7.9 %collective-permute-done.3 = bf16[1,1536,384]{2,1,0:T(8,128)(2,1)} collective-permute-done((bf16[1,1536,384]{2,1,0:T(8,128)(2,1)S(1)}, bf16[1,1536,384]{2,1,0:T(8,128)(2,1)}, u32[]{:S(2)}, u32[]{:S(2)}) %collective-permute-start.3) | collective-permute-done | bytes 1179680 | tf_op jit(solution)/shard_map/ppermute | solution.py:18
  99.8 2.6 copy.58
  102.5 7.9 %fusion.21 = f32[8,128]{1,0:T(8,128)S(1)} fusion(s32[3072]{0:T(1024)S(1)} %add_remainder_fusion, s32[3072]{0:T(1024)S(1)} %copy-done.10, s32[128]{0:T(128)S(1)} %copy-done.13, s32[8]{0:T(128)S(1)} %copy-done.12, pred[3072]{0:T(1024)(128)(4,1)S(1)} %copy-done.11), kind=kLoop, calls=%fused_computation.27 | loop fusion | flops 66059264 | bytes 32288 | tf_op jit(solution)/shard_map/reduce_sum | solution.py:69
  110.5 6.2 %maximum_select_fusion = bf16[768,3072]{1,0:T(8,128)(2,1)S(1)} fusion(bf16[768,1536]{1,0:T(8,128)(2,1)} %collective-permute-done.6, bf16[768,1536]{1,0:T(8,128)(2,1)} %bitcast.133, pred[]{:T(512)S(6)} %eq.5), kind=kLoop, calls=%fused_computation.49 | loop fusion | flops 21233664 | bytes 9437185 | tf_op jit(solution)/shard_map/jit(_where)/select_n | solution.py:127
  116.7 12.5 %fusion.45 = (bf16[1024,768]{1,0:T(8,128)(2,1)S(1)}, f32[1024,768]{1,0:T(8,128)}) fusion(bf16[1536,768]{0,1:T(8,128)(2,1)S(1)} %collective-permute-done.4, bf16[1536,768]{0,1:T(8,128)(2,1)S(1)} %bitcast.155, f32[1024]{0:T(1024)S(1)} %multiply_bitcast_fusion, s32[3072]{0:T(1024)S(1)} %add_remainder_fusion, s32[3072]{0:T(1024)S(1)} %copy-done.10, ...), kind=kOutput, calls=%fused_computation.66 | convolution fusion | flops 4908122112 | bytes 9473024 | tf_op jit(solution)/shard_map/dot_general | solution.py:139
  129.3 3.8 convolution_convert_fusion
  133.6 1.7 collective-permute-start.7
  135.3 1.8 convolution_convert_fusion.1
  137.2 44.5 %collective-permute-done.7 = bf16[1,2,2,128,2048]{4,3,2,1,0:T(8,128)(2,1)S(1)} collective-permute-done((bf16[1,2,2,128,2048]{4,3,2,1,0:T(8,128)(2,1)S(1)}, bf16[1,2,2,128,2048]{4,3,2,1,0:T(8,128)(2,1)S(1)}, u32[]{:S(2)}, u32[]{:S(2)}) %collective-permute-start.7) | collective-permute-done | bytes 2097184 | tf_op jit(solution)/shard_map/ppermute | solution.py:18
  183.3 3.3 collective-permute-start.11
  186.6 32.1 %collective-permute-done.8 = bf16[1,1,2,128,2048]{4,3,2,1,0:T(8,128)(2,1)S(1)} collective-permute-done((bf16[1,1,2,128,2048]{4,3,2,1,0:T(8,128)(2,1)S(1)}, bf16[1,1,2,128,2048]{4,3,2,1,0:T(8,128)(2,1)S(1)}, u32[]{:S(2)}, u32[]{:S(2)}) %collective-permute-start.8) | collective-permute-done | bytes 1048608 | tf_op jit(solution)/shard_map/ppermute | solution.py:18
  222.2 4.8 collective-permute-done.12
  227.1 16.8 %collective-permute-done.9 = bf16[1,1,1,128,2048]{4,3,2,1,0:T(8,128)(2,1)S(1)} collective-permute-done((bf16[1,1,1,128,2048]{4,3,2,1,0:T(8,128)(2,1)S(1)}, bf16[1,1,1,128,2048]{4,3,2,1,0:T(8,128)(2,1)S(1)}, u32[]{:S(2)}, u32[]{:S(2)}) %collective-permute-start.9) | collective-permute-done | bytes 524320 | tf_op jit(solution)/shard_map/ppermute | solution.py:18
  244.1 3.0 multiply_reduce_fusion
  247.1 2.0 multiply_convert_fusion.2
  249.1 1.6 collective-permute-start.14
  250.7 17.8 %collective-permute-done.14 = bf16[1,128,3072]{2,1,0:T(8,128)(2,1)S(1)} collective-permute-done((bf16[1,128,3072]{2,1,0:T(8,128)(2,1)S(1)}, bf16[1,128,3072]{2,1,0:T(8,128)(2,1)S(1)}, u32[]{:S(2)}, u32[]{:S(2)}) %collective-permute-start.14) | collective-permute-done | bytes 786464 | tf_op jit(solution)/shard_map/ppermute | solution.py:18
  268.7 3.4 collective-permute-done.15
  272.1 18.9 %convert_bitcast_fusion = bf16[3,2,256,1536]{3,2,0,1:T(8,128)(2,1)S(1)} fusion(bf16[1,3,3072,1536]{3,2,1,0:T(8,128)(2,1)} %param.10, bf16[1,256,3072]{2,1,0:T(8,128)(2,1)S(1)} %bitcast.170, bf16[1,256,3072]{2,1,0:T(8,128)(2,1)S(1)} %bitcast.165), kind=kOutput, calls=%fused_computation.54 | convolution fusion | flops 14504165376 | bytes 36175872 | tf_op jit(solution)/shard_map/bsd,kdh->kbsh/dot_general | solution.py:83
  292.5 1.6 copy.61
  294.1 1.7 copy.62
  295.8 1.8 copy.63
  297.6 2.9 fusion.28
  303.0 3.7 fusion.35
  306.8 3.5 collective-permute-done.16
  310.3 5.2 subtract_multiply_fusion
  315.6 1.6 collective-permute-start.17
  317.2 18.1 %collective-permute-done.17 = bf16[1,128,3072]{2,1,0:T(8,128)(2,1)S(1)} collective-permute-done((bf16[1,128,3072]{2,1,0:T(8,128)(2,1)S(1)}, bf16[1,128,3072]{2,1,0:T(8,128)(2,1)S(1)}, u32[]{:S(2)}, u32[]{:S(2)}) %collective-permute-start.17) | collective-permute-done | bytes 786464 | tf_op jit(solution)/shard_map/ppermute | solution.py:18
  335.6 24.6 %collective-permute-done.19 = bf16[1,1,1,128,2048]{4,3,2,1,0:T(8,128)(2,1)S(1)} collective-permute-done((bf16[1,1,1,128,2048]{4,3,2,1,0:T(8,128)(2,1)S(1)}, bf16[1,1,1,128,2048]{4,3,2,1,0:T(8,128)(2,1)S(1)}, u32[]{:S(2)}, u32[]{:S(2)}) %collective-permute-start.19) | collective-permute-done | bytes 524320 | tf_op jit(solution)/shard_map/ppermute | solution.py:18
  361.7 7.0 %collective-permute-done.22 = bf16[1,1,1,128,1024]{4,3,2,1,0:T(8,128)(2,1)S(1)} collective-permute-done((bf16[1,1,1,128,1024]{4,3,2,1,0:T(8,128)(2,1)S(1)}, bf16[1,1,1,128,1024]{4,3,2,1,0:T(8,128)(2,1)S(1)}, u32[]{:S(2)}, u32[]{:S(2)}) %collective-permute-start.22) | collective-permute-done | bytes 262176 | tf_op jit(solution)/shard_map/ppermute | solution.py:18
  368.7 2.2 collective-permute-start.23
  370.9 25.7 %collective-permute-done.20 = bf16[1,1,2,128,2048]{4,3,2,1,0:T(8,128)(2,1)S(1)} collective-permute-done((bf16[1,1,2,128,2048]{4,3,2,1,0:T(8,128)(2,1)S(1)}, bf16[1,1,2,128,2048]{4,3,2,1,0:T(8,128)(2,1)S(1)}, u32[]{:S(2)}, u32[]{:S(2)}) %collective-permute-start.20) | collective-permute-done | bytes 1048608 | tf_op jit(solution)/shard_map/ppermute | solution.py:18
  398.4 8.0 %fusion.22 = bf16[1024,3072]{1,0:T(8,128)(2,1)S(1)} fusion(f32[1024]{0:T(1024)S(1)} %multiply_bitcast_fusion, s32[3072]{0:T(1024)S(1)} %add_remainder_fusion, s32[3072]{0:T(1024)S(1)} %copy-done.10, s32[1024]{0:T(1024)S(1)} %add_bitcast_fusion, pred[3072]{0:T(1024)(128)(4,1)S(1)} %copy-done.11), kind=kLoop, calls=%fused_computation.28 | loop fusion | flops 59768832 | bytes 6327296 | tf_op jit(solution)/shard_map/convert_element_type | solution.py:137
  406.4 16.0 %collective-permute-done.24 = bf16[2,1,2,128,1024]{4,3,2,1,0:T(8,128)(2,1)S(1)} collective-permute-done((bf16[2,1,2,128,1024]{4,3,2,1,0:T(8,128)(2,1)S(1)}, bf16[2,1,2,128,1024]{4,3,2,1,0:T(8,128)(2,1)S(1)}, u32[]{:S(2)}, u32[]{:S(2)}) %collective-permute-start.24) | collective-permute-done | bytes 1048608 | tf_op jit(solution)/shard_map/ppermute | solution.py:18
  422.6 21.1 %collective-permute-done.21 = bf16[1,2,2,128,2048]{4,3,2,1,0:T(8,128)(2,1)S(1)} collective-permute-done((bf16[1,2,2,128,2048]{4,3,2,1,0:T(8,128)(2,1)S(1)}, bf16[1,2,2,128,2048]{4,3,2,1,0:T(8,128)(2,1)S(1)}, u32[]{:S(2)}, u32[]{:S(2)}) %collective-permute-start.21) | collective-permute-done | bytes 2097184 | tf_op jit(solution)/shard_map/ppermute | solution.py:18
  444.1 9.0 %fusion.52 = bf16[1024,768]{1,0:T(8,128)(2,1)S(1)} fusion(f32[1024,768]{1,0:T(8,128)} %get-tuple-element.20, bf16[768,3072]{1,0:T(8,128)(2,1)S(1)} %bitcast.142, bf16[1024,1024]{1,0:T(8,128)(2,1)S(1)} %bitcast.157, bf16[1024,2048]{1,0:T(8,128)(2,1)S(1)} %bitcast.150), kind=kOutput, calls=%fused_computation.73 | convolution fusion | flops 4859363328 | bytes 15728640 | tf_op jit(solution)/shard_map/dot_general | solution.py:198
  453.2 4.2 multiply_convert_fusion.1
  457.5 6.0 %multiply_convert_fusion = bf16[768,1536]{1,0:T(8,128)(2,1)} fusion(bf16[1024,768]{1,0:T(8,128)(2,1)} %copy-done.14, s32[]{:T(128)S(6)} %select_n.49, bf16[1024,2048]{1,0:T(8,128)(2,1)} %bitcast.151, bf16[1024,1024]{1,0:T(8,128)(2,1)S(1)} %bitcast.158), kind=kOutput, calls=%fused_computation.51 | convolution fusion | flops 2424569856 | bytes 10223620 | tf_op jit(solution)/shard_map/dot_general | solution.py:106
  464.5 5.3 add_convert_fusion.1
  469.8 3.0 copy.68
  474.0 1.5 collective-permute-start.26
  475.5 7.4 %add_convert_fusion = bf16[768,1536]{1,0:T(8,128)(2,1)} fusion(bf16[768,1536]{1,0:T(8,128)(2,1)} %collective-permute-done.27, bf16[1024,768]{1,0:T(8,128)(2,1)} %copy-done.14, s32[]{:T(128)S(6)} %select_n.48, bf16[1024,2048]{1,0:T(8,128)(2,1)} %bitcast.152, bf16[1024,1024]{1,0:T(8,128)(2,1)} %bitcast.159), kind=kOutput, calls=%fused_computation.50 | convolution fusion | flops 2426929152 | bytes 12582916 | tf_op jit(solution)/shard_map/dot_general | solution.py:106
  482.9 19.2 %collective-permute-done.26 = bf16[1,1536,384]{2,1,0:T(8,128)(2,1)} collective-permute-done((bf16[1,1536,384]{2,1,0:T(8,128)(2,1)}, bf16[1,1536,384]{2,1,0:T(8,128)(2,1)}, u32[]{:S(2)}, u32[]{:S(2)}) %collective-permute-start.26) | collective-permute-done | bytes 1179680 | tf_op jit(solution)/shard_map/ppermute | solution.py:18
  502.2 2.6 add_convert_fusion.2
  504.7 4.2 all-to-all-start.2
  510.4 1.6 collective-permute-start.28
  512.0 25.3 %collective-permute-done.28 = bf16[1,384,1536]{2,1,0:T(8,128)(2,1)S(1)} collective-permute-done((bf16[1,384,1536]{2,1,0:T(8,128)(2,1)S(1)}, bf16[1,384,1536]{2,1,0:T(8,128)(2,1)S(1)}, u32[]{:S(2)}, u32[]{:S(2)}) %collective-permute-start.28) | collective-permute-done | bytes 1179680 | tf_op jit(solution)/shard_map/ppermute | solution.py:18
  539.0 5.7 all-to-all-start.3
  545.7 1.6 collective-permute-start.13
  548.2 1.8 bitcast_dynamic-update-slice_fusion.2
  552.2 4.7 collective-permute-done.13
  557.7 4.9 collective-permute-done.18
  564.6 6.7 %all-to-all-done.3 = bf16[384,8,192]{0,2,1:T(8,128)(2,1)S(1)} async-done(((bf16[384,8,192]{0,2,1:T(8,128)(2,1)}), bf16[384,8,192]{0,2,1:T(8,128)(2,1)S(1)}, u32[]{:S(2)}, u32[]{:S(2)}) %all-to-all-start.3) | async-done | bytes 1179680 | tf_op jit(solution)/shard_map/all_to_all | solution.py:196
  (128 shorter events, 37.5 us)
Async XLA Ops:
  0.6 9.8 %copy-start.9 = (bf16[192,3072]{1,0:T(8,128)(2,1)S(1)}, bf16[192,3072]{1,0:T(8,128)(2,1)}, u32[]{:S(2)}) copy-start(bf16[192,3072]{1,0:T(8,128)(2,1)} %param.8) | copy-start | bytes 3538948
  3.1 35.8 %all-to-all-start.1 = ((bf16[8,384,192]{1,2,0:T(8,128)(2,1)}), bf16[8,384,192]{1,2,0:T(8,128)(2,1)S(1)}, u32[]{:S(2)}, u32[]{:S(2)}) async-start(bf16[8,384,192]{1,2,0:T(8,128)(2,1)} %bitcast.123), calls=%async_computation.1 | async-start | bytes 2359296 | tf_op jit(solution)/shard_map/all_to_all | solution.py:120
  39.0 46.1 %copy-start.3 = (bf16[8,384,192]{1,2,0:T(8,128)(2,1)}, bf16[8,384,192]{1,2,0:T(8,128)(2,1)S(1)}, u32[]{:S(2)}) copy-start(bf16[8,384,192]{1,2,0:T(8,128)(2,1)S(1)} %all-to-all-done.1) | copy-start | bytes 3538948
  39.0 32.4 %all-to-all-start = ((bf16[192,8,384]{2,0,1:T(8,128)(2,1)}), bf16[192,8,384]{2,0,1:T(8,128)(2,1)S(1)}, u32[]{:S(2)}, u32[]{:S(2)}) async-start(bf16[192,8,384]{2,0,1:T(8,128)(2,1)} %bitcast.124), calls=%async_computation | async-start | bytes 2359296 | tf_op jit(solution)/shard_map/all_to_all | solution.py:119
  42.6 42.4 %collective-permute-start.5 = (bf16[1,384,1536]{1,2,0:T(8,128)(2,1)S(1)}, bf16[1,384,1536]{1,2,0:T(8,128)(2,1)}, u32[]{:S(2)}, u32[]{:S(2)}) collective-permute-start(bf16[1,384,1536]{1,2,0:T(8,128)(2,1)S(1)} %bitcast.148), channel_id=1, source_target_pairs={{0,1},{1,0},{2,3},{3,2},{4,5},{5,4},{6,7},{7,6},{8,9},{9,8},{10,11... | collective-permute-start | bytes 3538952 | tf_op jit(solution)/shard_map/ppermute | solution.py:18
  44.2 29.9 %collective-permute-start = (s32[1,1,1,1]{2,1,0,3:T(1,128)}, s32[1,1,1,1]{2,1,0,3:T(1,128)}, u32[]{:S(2)}, u32[]{:S(2)}) collective-permute-start(s32[1,1,1,1]{2,1,0,3:T(1,128)} %bitcast.1), channel_id=1, source_target_pairs={{0,2},{2,0},{4,6},{6,4},{8,10},{10,8},{12,14},{14,12},{1,3},{3,1},... | collective-permute-start | bytes 20 | tf_op jit(solution)/shard_map/ppermute | solution.py:18
  71.4 26.9 %collective-permute-start.3 = (bf16[1,1536,384]{2,1,0:T(8,128)(2,1)S(1)}, bf16[1,1536,384]{2,1,0:T(8,128)(2,1)}, u32[]{:S(2)}, u32[]{:S(2)}) collective-permute-start(bf16[1,1536,384]{2,1,0:T(8,128)(2,1)S(1)} %bitcast.146), channel_id=1, source_target_pairs={{0,1},{1,0},{2,3},{3,2},{4,5},{5,4},{6,7},{7,6},{8,9},{9,8},{10,11... | collective-permute-start | bytes 3538952 | tf_op jit(solution)/shard_map/ppermute | solution.py:18
  74.7 3.6 collective-permute-start.1
  79.1 4.5 collective-permute-start.2
  89.6 20.9 %collective-permute-start.6 = (bf16[768,1536]{1,0:T(8,128)(2,1)}, bf16[768,1536]{1,0:T(8,128)(2,1)}, u32[]{:S(2)}, u32[]{:S(2)}) collective-permute-start(bf16[768,1536]{1,0:T(8,128)(2,1)} %bitcast.132), channel_id=1, source_target_pairs={{0,16},{16,0},{1,17},{17,1},{2,18},{18,2},{3,19},{19,3},{4,20},{20... | collective-permute-start | bytes 7077896 | tf_op jit(solution)/shard_map/ppermute | solution.py:18
  99.8 2.7 copy-start.10
  99.8 2.7 copy-start.11
  99.8 2.7 copy-start.12
  99.8 2.7 copy-start.13
  102.5 14.2 %collective-permute-start.4 = (bf16[1536,768]{0,1:T(8,128)(2,1)}, bf16[1536,768]{0,1:T(8,128)(2,1)S(1)}, u32[]{:S(2)}, u32[]{:S(2)}) collective-permute-start(bf16[1536,768]{0,1:T(8,128)(2,1)} %bitcast.154), channel_id=1, source_target_pairs={{0,16},{16,0},{1,17},{17,1},{2,18},{18,2},{3,19},{19,3},{4,20},{20... | collective-permute-start | bytes 7077896 | tf_op jit(solution)/shard_map/ppermute | solution.py:18
  110.5 6.2 %copy-start.6 = (bf16[1536,2,384]{0,2,1:T(8,128)(2,1)S(1)}, bf16[1536,2,384]{0,2,1:T(8,128)(2,1)}, u32[]{:S(2)}) copy-start(bf16[1536,2,384]{0,2,1:T(8,128)(2,1)} %copy.58) | copy-start | bytes 7077892
  116.7 18.6 %copy-start.2 = (bf16[768,3072]{1,0:T(8,128)(2,1)}, bf16[768,3072]{1,0:T(8,128)(2,1)S(1)}, u32[]{:S(2)}) copy-start(bf16[768,3072]{1,0:T(8,128)(2,1)S(1)} %maximum_select_fusion) | copy-start | bytes 14155780
  129.3 6.0 %copy-start.14 = (bf16[1024,768]{1,0:T(8,128)(2,1)}, bf16[1024,768]{1,0:T(8,128)(2,1)S(1)}, u32[]{:S(2)}) copy-start(bf16[1024,768]{1,0:T(8,128)(2,1)S(1)} %get-tuple-element.19) | copy-start | bytes 4718596
  133.6 48.1 %collective-permute-start.7 = (bf16[1,2,2,128,2048]{4,3,2,1,0:T(8,128)(2,1)S(1)}, bf16[1,2,2,128,2048]{4,3,2,1,0:T(8,128)(2,1)S(1)}, u32[]{:S(2)}, u32[]{:S(2)}) collective-permute-start(bf16[1,2,2,128,2048]{4,3,2,1,0:T(8,128)(2,1)S(1)} %bitcast.162), channel_id=1, source_target_pairs={{0,2},{2,0},{4,6},{6,4},{8,10},{10,8},{12,14},{14,12},{1,3},{3,1},... | collective-permute-start | bytes 6291464 | tf_op jit(solution)/shard_map/ppermute | solution.py:18
  137.1 45.7 %collective-permute-start.10 = (bf16[2,1,2,128,1024]{4,3,2,1,0:T(8,128)(2,1)S(1)}, bf16[2,1,2,128,1024]{4,3,2,1,0:T(8,128)(2,1)S(1)}, u32[]{:S(2)}, u32[]{:S(2)}) collective-permute-start(bf16[2,1,2,128,1024]{4,3,2,1,0:T(8,128)(2,1)S(1)} %slice.147), channel_id=1, source_target_pairs={{0,4},{2,6},{4,0},{6,2},{8,12},{10,14},{12,8},{14,10},{1,5},{3,7},... | collective-permute-start | bytes 3145736 | tf_op jit(solution)/shard_map/ppermute | solution.py:18
  182.6 36.1 %collective-permute-start.8 = (bf16[1,1,2,128,2048]{4,3,2,1,0:T(8,128)(2,1)S(1)}, bf16[1,1,2,128,2048]{4,3,2,1,0:T(8,128)(2,1)S(1)}, u32[]{:S(2)}, u32[]{:S(2)}) collective-permute-start(bf16[1,1,2,128,2048]{4,3,2,1,0:T(8,128)(2,1)S(1)} %slice.207), channel_id=1, source_target_pairs={{0,4},{2,6},{4,0},{6,2},{8,12},{10,14},{12,8},{14,10},{1,5},{3,7},... | collective-permute-start | bytes 3145736 | tf_op jit(solution)/shard_map/ppermute | solution.py:18
  183.3 36.8 %collective-permute-start.11 = (bf16[2,1,1,128,1024]{4,3,2,1,0:T(8,128)(2,1)S(1)}, bf16[2,1,1,128,1024]{4,3,2,1,0:T(8,128)(2,1)S(1)}, u32[]{:S(2)}, u32[]{:S(2)}) collective-permute-start(bf16[2,1,1,128,1024]{4,3,2,1,0:T(8,128)(2,1)S(1)} %slice.208), channel_id=1, source_target_pairs={{0,8},{2,10},{4,12},{6,14},{8,0},{10,2},{12,4},{14,6},{1,9},{3,11}... | collective-permute-start | bytes 1572872 | tf_op jit(solution)/shard_map/ppermute | solution.py:18
  219.1 24.8 %collective-permute-start.9 = (bf16[1,1,1,128,2048]{4,3,2,1,0:T(8,128)(2,1)S(1)}, bf16[1,1,1,128,2048]{4,3,2,1,0:T(8,128)(2,1)S(1)}, u32[]{:S(2)}, u32[]{:S(2)}) collective-permute-start(bf16[1,1,1,128,2048]{4,3,2,1,0:T(8,128)(2,1)S(1)} %slice.209), channel_id=1, source_target_pairs={{0,8},{2,10},{4,12},{6,14},{8,0},{10,2},{12,4},{14,6},{1,9},{3,11}... | collective-permute-start | bytes 1572872 | tf_op jit(solution)/shard_map/ppermute | solution.py:18
  220.2 6.8 %collective-permute-start.12 = (bf16[1,1,1,128,1024]{4,3,2,1,0:T(8,128)(2,1)S(1)}, bf16[1,1,1,128,1024]{4,3,2,1,0:T(8,128)(2,1)S(1)}, u32[]{:S(2)}, u32[]{:S(2)}) collective-permute-start(bf16[1,1,1,128,1024]{4,3,2,1,0:T(8,128)(2,1)S(1)} %slice.210), channel_id=1, source_target_pairs={{0,2},{2,0},{4,6},{6,4},{8,10},{10,8},{12,14},{14,12},{1,3},{3,1},... | collective-permute-start | bytes 786440 | tf_op jit(solution)/shard_map/ppermute | solution.py:18
  249.1 19.4 %collective-permute-start.14 = (bf16[1,128,3072]{2,1,0:T(8,128)(2,1)S(1)}, bf16[1,128,3072]{2,1,0:T(8,128)(2,1)S(1)}, u32[]{:S(2)}, u32[]{:S(2)}) collective-permute-start(bf16[1,128,3072]{2,1,0:T(8,128)(2,1)S(1)} %multiply_convert_fusion.2), channel_id=1, source_target_pairs={{0,1},{1,0},{2,3},{3,2},{4,5},{5,4},{6,7},{7,6},{8,9},{9,8},{10,11... | collective-permute-start | bytes 2359304 | tf_op jit(solution)/shard_map/ppermute | solution.py:18
  268.6 3.5 collective-permute-start.15
  297.6 2.9 copy-start.8
  297.6 4.4 slice-start
  300.5 2.2 slice-start.1
  300.5 2.5 slice-start.2
  306.7 3.6 collective-permute-start.16
  315.6 19.6 %collective-permute-start.17 = (bf16[1,128,3072]{2,1,0:T(8,128)(2,1)S(1)}, bf16[1,128,3072]{2,1,0:T(8,128)(2,1)S(1)}, u32[]{:S(2)}, u32[]{:S(2)}) collective-permute-start(bf16[1,128,3072]{2,1,0:T(8,128)(2,1)S(1)} %fusion.113), channel_id=1, source_target_pairs={{0,1},{1,0},{2,3},{3,2},{4,5},{5,4},{6,7},{7,6},{8,9},{9,8},{10,11... | collective-permute-start | bytes 2359304 | tf_op jit(solution)/shard_map/ppermute | solution.py:18
  335.5 24.7 %collective-permute-start.19 = (bf16[1,1,1,128,2048]{4,3,2,1,0:T(8,128)(2,1)S(1)}, bf16[1,1,1,128,2048]{4,3,2,1,0:T(8,128)(2,1)S(1)}, u32[]{:S(2)}, u32[]{:S(2)}) collective-permute-start(bf16[1,1,1,128,2048]{4,3,2,1,0:T(8,128)(2,1)S(1)} %slice_bitcast_fusion.3), channel_id=1, source_target_pairs={{0,8},{2,10},{4,12},{6,14},{8,0},{10,2},{12,4},{14,6},{1,9},{3,11}... | collective-permute-start | bytes 1572872 | tf_op jit(solution)/shard_map/ppermute | solution.py:18
  360.3 36.4 %collective-permute-start.20 = (bf16[1,1,2,128,2048]{4,3,2,1,0:T(8,128)(2,1)S(1)}, bf16[1,1,2,128,2048]{4,3,2,1,0:T(8,128)(2,1)S(1)}, u32[]{:S(2)}, u32[]{:S(2)}) collective-permute-start(bf16[1,1,2,128,2048]{4,3,2,1,0:T(8,128)(2,1)S(1)} %pad_maximum_fusion.9), channel_id=1, source_target_pairs={{0,4},{2,6},{4,0},{6,2},{8,12},{10,14},{12,8},{14,10},{1,5},{3,7},... | collective-permute-start | bytes 3145736 | tf_op jit(solution)/shard_map/ppermute | solution.py:18
  360.4 8.3 %collective-permute-start.22 = (bf16[1,1,1,128,1024]{4,3,2,1,0:T(8,128)(2,1)S(1)}, bf16[1,1,1,128,1024]{4,3,2,1,0:T(8,128)(2,1)S(1)}, u32[]{:S(2)}, u32[]{:S(2)}) collective-permute-start(bf16[1,1,1,128,1024]{4,3,2,1,0:T(8,128)(2,1)S(1)} %slice_bitcast_fusion.4), channel_id=1, source_target_pairs={{0,2},{2,0},{4,6},{6,4},{8,10},{10,8},{12,14},{14,12},{1,3},{3,1},... | collective-permute-start | bytes 786440 | tf_op jit(solution)/shard_map/ppermute | solution.py:18
  368.7 29.5 %collective-permute-start.23 = (bf16[2,1,1,128,1024]{4,3,2,1,0:T(8,128)(2,1)S(1)}, bf16[2,1,1,128,1024]{4,3,2,1,0:T(8,128)(2,1)S(1)}, u32[]{:S(2)}, u32[]{:S(2)}) collective-permute-start(bf16[2,1,1,128,1024]{4,3,2,1,0:T(8,128)(2,1)S(1)} %pad_maximum_fusion.11), channel_id=1, source_target_pairs={{0,8},{2,10},{4,12},{6,14},{8,0},{10,2},{12,4},{14,6},{1,9},{3,11}... | collective-permute-start | bytes 1572872 | tf_op jit(solution)/shard_map/ppermute | solution.py:18
  396.9 46.8 %collective-permute-start.21 = (bf16[1,2,2,128,2048]{4,3,2,1,0:T(8,128)(2,1)S(1)}, bf16[1,2,2,128,2048]{4,3,2,1,0:T(8,128)(2,1)S(1)}, u32[]{:S(2)}, u32[]{:S(2)}) collective-permute-start(bf16[1,2,2,128,2048]{4,3,2,1,0:T(8,128)(2,1)S(1)} %pad_maximum_fusion.4), channel_id=1, source_target_pairs={{0,2},{2,0},{4,6},{6,4},{8,10},{10,8},{12,14},{14,12},{1,3},{3,1},... | collective-permute-start | bytes 6291464 | tf_op jit(solution)/shard_map/ppermute | solution.py:18
  398.3 24.0 %collective-permute-start.24 = (bf16[2,1,2,128,1024]{4,3,2,1,0:T(8,128)(2,1)S(1)}, bf16[2,1,2,128,1024]{4,3,2,1,0:T(8,128)(2,1)S(1)}, u32[]{:S(2)}, u32[]{:S(2)}) collective-permute-start(bf16[2,1,2,128,1024]{4,3,2,1,0:T(8,128)(2,1)S(1)} %pad_maximum_fusion.10), channel_id=1, source_target_pairs={{0,4},{2,6},{4,0},{6,2},{8,12},{10,14},{12,8},{14,10},{1,5},{3,7},... | collective-permute-start | bytes 3145736 | tf_op jit(solution)/shard_map/ppermute | solution.py:18
  406.4 46.8 %copy-start = (bf16[1024,3072]{1,0:T(8,128)(2,1)}, bf16[1024,3072]{1,0:T(8,128)(2,1)S(1)}, u32[]{:S(2)}) copy-start(bf16[1024,3072]{1,0:T(8,128)(2,1)S(1)} %fusion.22) | copy-start | bytes 18874372
  422.3 21.8 %slice-start.3 = ((s8[4718592]{0:T(1024)(128)(4,1)}), s8[4194304]{0:T(1024)(128)(4,1)S(1)}, s32[]{:S(2)}) async-start(s8[4718592]{0:T(1024)(128)(4,1)} %bitcast.141), calls=%async_computation.7 | async-start | bytes 8388608
  422.5 34.9 %copy-start.7 = (bf16[2,2,2,128,1024]{4,3,2,1,0:T(8,128)(2,1)}, bf16[2,2,2,128,1024]{4,3,2,1,0:T(8,128)(2,1)S(1)}, u32[]{:S(2)}) copy-start(bf16[2,2,2,128,1024]{4,3,2,1,0:T(8,128)(2,1)S(1)} %pad_maximum_fusion.5) | copy-start | bytes 6291460
  422.6 21.6 %slice-start.4 = ((s8[4718592]{0:T(1024)(128)(4,1)}), s8[524288]{0:T(1024)(128)(4,1)S(1)}, s32[]{:S(2)}) async-start(s8[4718592]{0:T(1024)(128)(4,1)} %bitcast.141), calls=%async_computation.8 | async-start | bytes 1048576
  444.1 9.0 %copy-start.4 = (bf16[2,2,2,128,2048]{4,3,2,1,0:T(8,128)(2,1)}, bf16[2,2,2,128,2048]{4,3,2,1,0:T(8,128)(2,1)S(1)}, u32[]{:S(2)}) copy-start(bf16[2,2,2,128,2048]{4,3,2,1,0:T(8,128)(2,1)S(1)} %pad_maximum_fusion.2) | copy-start | bytes 12582916
  453.1 4.2 copy-start.15
  457.4 7.2 %collective-permute-start.25 = (bf16[1536,768]{0,1:T(8,128)(2,1)}, bf16[1536,768]{0,1:T(8,128)(2,1)}, u32[]{:S(2)}, u32[]{:S(2)}) collective-permute-start(bf16[1536,768]{0,1:T(8,128)(2,1)} %multiply_convert_fusion.1), channel_id=1, source_target_pairs={{0,16},{16,0},{1,17},{17,1},{2,18},{18,2},{3,19},{19,3},{4,20},{20... | collective-permute-start | bytes 7077896 | tf_op jit(solution)/shard_map/ppermute | solution.py:18
  457.5 7.1 %copy-start.1 = (bf16[1024,3072]{1,0:T(8,128)(2,1)S(1)}, bf16[1024,3072]{1,0:T(8,128)(2,1)}, u32[]{:S(2)}) copy-start(bf16[1024,3072]{1,0:T(8,128)(2,1)} %copy-done) | copy-start | bytes 18874372
  457.5 7.1 %copy-start.16 = (bf16[1024,768]{1,0:T(8,128)(2,1)S(1)}, bf16[1024,768]{1,0:T(8,128)(2,1)}, u32[]{:S(2)}) copy-start(bf16[1024,768]{1,0:T(8,128)(2,1)} %copy-done.15) | copy-start | bytes 4718596
  463.5 12.0 %collective-permute-start.27 = (bf16[768,1536]{1,0:T(8,128)(2,1)}, bf16[768,1536]{1,0:T(8,128)(2,1)}, u32[]{:S(2)}, u32[]{:S(2)}) collective-permute-start(bf16[768,1536]{1,0:T(8,128)(2,1)} %multiply_convert_fusion), channel_id=1, source_target_pairs={{0,16},{16,0},{1,17},{17,1},{2,18},{18,2},{3,19},{19,3},{4,20},{20... | collective-permute-start | bytes 7077896 | tf_op jit(solution)/shard_map/ppermute | solution.py:18
  474.0 28.2 %collective-permute-start.26 = (bf16[1,1536,384]{2,1,0:T(8,128)(2,1)}, bf16[1,1536,384]{2,1,0:T(8,128)(2,1)}, u32[]{:S(2)}, u32[]{:S(2)}) collective-permute-start(bf16[1,1536,384]{2,1,0:T(8,128)(2,1)} %slice.164), channel_id=1, source_target_pairs={{0,1},{1,0},{2,3},{3,2},{4,5},{5,4},{6,7},{7,6},{8,9},{9,8},{10,11... | collective-permute-start | bytes 3538952 | tf_op jit(solution)/shard_map/ppermute | solution.py:18
  504.7 34.2 %all-to-all-start.2 = ((bf16[8,192,384]{2,1,0:T(8,128)(2,1)}), bf16[8,192,384]{2,1,0:T(8,128)(2,1)S(1)}, u32[]{:S(2)}, u32[]{:S(2)}) async-start(bf16[8,192,384]{2,1,0:T(8,128)(2,1)} %bitcast.140), calls=%async_computation.2 | async-start | bytes 2359296 | tf_op jit(solution)/shard_map/all_to_all | solution.py:209
  508.9 28.3 %copy-start.5 = (bf16[768,1536]{1,0:T(8,128)(2,1)S(1)}, bf16[768,1536]{1,0:T(8,128)(2,1)}, u32[]{:S(2)}) copy-start(bf16[768,1536]{1,0:T(8,128)(2,1)} %add_convert_fusion) | copy-start | bytes 7077892
  510.4 26.8 %collective-permute-start.28 = (bf16[1,384,1536]{2,1,0:T(8,128)(2,1)S(1)}, bf16[1,384,1536]{2,1,0:T(8,128)(2,1)S(1)}, u32[]{:S(2)}, u32[]{:S(2)}) collective-permute-start(bf16[1,384,1536]{2,1,0:T(8,128)(2,1)S(1)} %slice_bitcast_fusion.1), channel_id=1, source_target_pairs={{0,1},{1,0},{2,3},{3,2},{4,5},{5,4},{6,7},{7,6},{8,9},{9,8},{10,11... | collective-permute-start | bytes 3538952 | tf_op jit(solution)/shard_map/ppermute | solution.py:18
  539.0 32.4 %all-to-all-start.3 = ((bf16[384,8,192]{0,2,1:T(8,128)(2,1)}), bf16[384,8,192]{0,2,1:T(8,128)(2,1)S(1)}, u32[]{:S(2)}, u32[]{:S(2)}) async-start(bf16[384,8,192]{0,2,1:T(8,128)(2,1)} %bitcast.144), calls=%async_computation.3 | async-start | bytes 2359296 | tf_op jit(solution)/shard_map/all_to_all | solution.py:196
  545.7 11.2 %collective-permute-start.13 = (bf16[128,1536]{1,0:T(8,128)(2,1)S(1)}, bf16[128,1536]{1,0:T(8,128)(2,1)S(1)}, u32[]{:S(2)}, u32[]{:S(2)}) collective-permute-start(bf16[128,1536]{1,0:T(8,128)(2,1)S(1)} %constant_dynamic-slice_fusion), channel_id=1, source_target_pairs={{0,1},{1,0},{2,3},{3,2},{4,5},{5,4},{6,7},{7,6},{8,9},{9,8},{10,11... | collective-permute-start | bytes 1179656 | tf_op jit(solution)/shard_map/ppermute | solution.py:18
  551.7 10.9 %collective-permute-start.18 = (bf16[128,1536]{1,0:T(8,128)(2,1)S(1)}, bf16[128,1536]{1,0:T(8,128)(2,1)S(1)}, u32[]{:S(2)}, u32[]{:S(2)}) collective-permute-start(bf16[128,1536]{1,0:T(8,128)(2,1)S(1)} %get-tuple-element.17), channel_id=1, source_target_pairs={{0,1},{1,0},{2,3},{3,2},{4,5},{5,4},{6,7},{7,6},{8,9},{9,8},{10,11... | collective-permute-start | bytes 1179656 | tf_op jit(solution)/shard_map/ppermute | solution.py:18

commit v2 on v1

--- a/solution.py
+++ b/solution.py
@@ -1,6 +1,10 @@
+import functools
+
 import jax
 import jax.numpy as jnp
 from jax import lax
+from jax.experimental import pallas as pl
+from jax.experimental.pallas import tpu as pltpu
 from jax.sharding import PartitionSpec as P
 
 D = 3072
@@ -63,6 +67,253 @@
     mixing = mixing ^ mixing >> 16
     level = (mixing >> 7 & 65535).astype(jnp.float32)
     return ((level + 0.5) * (2.0 / 65536.0) - 1.0) * ROOT_THREE
+
+
+ROWS = 16
+
+
+def greet(spot, line, pair):
+    barrier = pltpu.get_barrier_semaphore()
+
+    def signal(to):
+        pl.semaphore_signal(
+            barrier, inc=1, device_id={"dp": to}, device_id_type=pl.DeviceIdType.MESH
+        )
+
+    me = lax.axis_index("dp")
+    signal(pair)
+
+    @pl.when(spot > 0)
+    def _():
+        signal(me - 2)
+
+    @pl.when(spot < line - 1)
+    def _():
+        signal(me + 2)
+
+    ends = (spot == 0).astype(jnp.int32) + (spot == line - 1).astype(jnp.int32)
+    pl.semaphore_wait(barrier, 3 - ends)
+
+
+def remote(source, target, send_sem, recv_sem, to):
+    return pltpu.make_async_remote_copy(
+        src_ref=source,
+        dst_ref=target,
+        send_sem=send_sem,
+        recv_sem=recv_sem,
+        device_id={"dp": to},
+        device_id_type=pl.DeviceIdType.MESH,
+    )
+
+
+def sum_kernel(line, parts, out, paired, lower, upper, p_send, p_recv, l_send, l_recv, u_send, u_recv):
+    me = lax.axis_index("dp")
+    side, spot = lax.rem(me, 2), lax.div(me, 2)
+    pair = me + 1 - 2 * side
+    steps = parts.shape[1] // ROWS
+    greet(spot, line, pair)
+
+    def to_pair(d):
+        return remote(parts.at[2 * d + 1 - side], paired.at[d], p_send.at[d], p_recv.at[d], pair)
+
+    def to_next(d):
+        return remote(paired.at[d], lower.at[d], l_send.at[d], l_recv.at[d], me + 2)
+
+    def to_last(d):
+        return remote(paired.at[d], upper.at[d], u_send.at[d], u_recv.at[d], me - 2)
+
+    def add(target, d, terms):
+        @pl.loop(0, steps)
+        def _(step):
+            rows = pl.ds(pl.multiple_of(step * ROWS, ROWS), ROWS)
+            total = parts[2 * d + side, rows].astype(jnp.float32)
+            for term in terms:
+                total = total + term[d, rows].astype(jnp.float32)
+            if target is out:
+                out[rows] = total
+            else:
+                target[d, rows] = total.astype(jnp.bfloat16)
+
+    for far in range(line - 1, 0, -1):
+
+        @pl.when(spot + far < line)
+        def _():
+            to_pair(spot + far).start()
+
+        @pl.when(spot - far >= 0)
+        def _():
+            to_pair(spot - far).start()
+
+    to_pair(spot).start()
+
+    for far in range(line - 1, 0, -1):
+        up, down = spot + far, spot - far
+
+        @pl.when(up < line)
+        def _():
+            to_pair(up).wait_recv()
+
+            @pl.when(spot > 0)
+            def _():
+                to_next(up).wait_recv()
+                add(paired, up, (paired, lower))
+
+            @pl.when(spot == 0)
+            def _():
+                add(paired, up, (paired,))
+
+            to_next(up).start()
+
+        @pl.when(down >= 0)
+        def _():
+            to_pair(down).wait_recv()
+
+            @pl.when(spot < line - 1)
+            def _():
+                to_last(down).wait_recv()
+                add(paired, down, (paired, upper))
+
+            @pl.when(spot == line - 1)
+            def _():
+                add(paired, down, (paired,))
+
+            to_last(down).start()
+
+    to_pair(spot).wait_recv()
+
+    @pl.when(spot == 0)
+    def _():
+        to_last(spot).wait_recv()
+        add(out, spot, (paired, upper))
+
+    @pl.when(spot == line - 1)
+    def _():
+        to_next(spot).wait_recv()
+        add(out, spot, (paired, lower))
+
+    @pl.when((spot > 0) & (spot < line - 1))
+    def _():
+        to_next(spot).wait_recv()
+        to_last(spot).wait_recv()
+        add(out, spot, (paired, lower, upper))
+
+    for d in range(line):
+        to_pair(d).wait_send()
+
+        @pl.when(d > spot)
+        def _():
+            to_next(d).wait_send()
+
+        @pl.when(d < spot)
+        def _():
+            to_last(d).wait_send()
+
+
+def sum_over_dp(parts):
+    line = parts.shape[0] // 2
+    block = parts.shape[1:]
+    slots = pltpu.VMEM((line,) + block, jnp.bfloat16)
+    return pl.pallas_call(
+        functools.partial(sum_kernel, line),
+        out_shape=jax.ShapeDtypeStruct(block, jnp.float32),
+        in_specs=[pl.BlockSpec(memory_space=pltpu.VMEM)],
+        out_specs=pl.BlockSpec(memory_space=pltpu.VMEM),
+        scratch_shapes=[slots] * 3 + [pltpu.SemaphoreType.DMA((line,))] * 6,
+        compiler_params=pltpu.CompilerParams(
+            collective_id=0, has_side_effects=True, vmem_limit_bytes=40 << 20
+        ),
+        cost_estimate=pl.CostEstimate(
+            flops=2 * parts.size, bytes_accessed=40 * parts.size, transcendentals=0
+        ),
+    )(parts)
+
+
+def gather_kernel(line, own, out, own_sem, recv, p_send, n_send, l_send):
+    me = lax.axis_index("dp")
+    side, spot = lax.rem(me, 2), lax.div(me, 2)
+    pair = me + 1 - 2 * side
+    greet(spot, line, pair)
+
+    def source(d, first):
+        return own if first else out.at[2 * d + side]
+
+    def move(d, sems, to, first=False):
+        b = 2 * d + side
+        return remote(source(d, first), out.at[b], sems.at[d], recv.at[b], to)
+
+    def arrived(b):
+        remote(out.at[b], out.at[b], p_send.at[0], recv.at[b], pair).wait_recv()
+
+    kept = pltpu.make_async_copy(own, out.at[me], own_sem)
+
+    @pl.when(spot < line - 1)
+    def _():
+        move(spot, n_send, me + 2, True).start()
+
+    @pl.when(spot > 0)
+    def _():
+        move(spot, l_send, me - 2, True).start()
+
+    move(spot, p_send, pair, True).start()
+    kept.start()
+    for far in range(1, line):
+        low, high = spot - far, spot + far
+
+        @pl.when(low >= 0)
+        def _():
+            arrived(2 * low + side)
+
+            @pl.when(spot < line - 1)
+            def _():
+                move(low, n_send, me + 2).start()
+
+            move(low, p_send, pair).start()
+
+        @pl.when(high < line)
+        def _():
+            arrived(2 * high + side)
+
+            @pl.when(spot > 0)
+            def _():
+                move(high, l_send, me - 2).start()
+
+            move(high, p_send, pair).start()
+
+    for d in range(line):
+        arrived(2 * d + 1 - side)
+        move(d, p_send, pair).wait_send()
+
+        @pl.when((d <= spot) & (spot < line - 1))
+        def _():
+            move(d, n_send, me + 2).wait_send()
+
+        @pl.when((d >= spot) & (spot > 0))
+        def _():
+            move(d, l_send, me - 2).wait_send()
+
+    kept.wait()
+
+
+def gather_over_dp(own):
+    count = lax.axis_size("dp")
+    line = count // 2
+    return pl.pallas_call(
+        functools.partial(gather_kernel, line),
+        out_shape=jax.ShapeDtypeStruct((count,) + own.shape, own.dtype),
+        in_specs=[pl.BlockSpec(memory_space=pl.ANY)],
+        out_specs=pl.BlockSpec(memory_space=pl.ANY),
+        scratch_shapes=[
+            pltpu.SemaphoreType.DMA(()),
+            pltpu.SemaphoreType.DMA((count,)),
+            pltpu.SemaphoreType.DMA((line,)),
+            pltpu.SemaphoreType.DMA((line,)),
+            pltpu.SemaphoreType.DMA((line,)),
+        ],
+        compiler_params=pltpu.CompilerParams(collective_id=1, has_side_effects=True),
+        cost_estimate=pl.CostEstimate(
+            flops=0, bytes_accessed=40 * count * own.size, transcendentals=0
+        ),
+    )(own)
 
 
 def rms_norm(value):
@@ -110,13 +361,12 @@
     n_dp, n_mp = lax.axis_size("dp"), lax.axis_size("mp")
     batch_size = lax.axis_size("group") * n_dp
     group, mp = lax.axis_index("group"), lax.axis_index("mp")
-    dp_bits, mp_bits = bits_of("dp"), bits_of("mp")
-    near_first = dp_bits
-    far_first = dp_bits[1:] + dp_bits[:1]
+    mp_bits = bits_of("mp")
     length = SEQ // n_mp
     half = D // 2
 
     up = lax.all_to_all(gen_up, "dp", split_axis=1, concat_axis=0, tiled=True)
+    gen_down, up = lax.optimization_barrier((gen_down, up))
     down = lax.all_to_all(gen_down, "dp", split_axis=0, concat_axis=1, tiled=True)
     share = up.shape[1]
     up = xor_gather(up, "mp", mp_bits).reshape(n_mp, half, share)
@@ -130,7 +380,7 @@
         jnp.concatenate([down_other, down], axis=1),
     )
 
-    seeds = xor_gather(noise_seeds, "dp", near_first).reshape(n_dp, 1, 1)
+    seeds = lax.all_gather(noise_seeds, "dp", tiled=True)[:, None, None]
     shape = (n_dp, length, D)
     tokens = lax.broadcasted_iota(jnp.int32, shape, 1) + mp * length
     feature = (lax.broadcasted_iota(jnp.int32, shape, 2) + group * half) % D
@@ -139,19 +389,8 @@
     before = jnp.dot(normed, up, preferred_element_type=jnp.float32)
     hidden = jax.nn.gelu(before, approximate=True).astype(jnp.bfloat16)
 
-    def stacked(value):
-        return value.reshape((2,) * len(dp_bits) + (length, value.shape[-1]))
-
-    cut = D * 2 // 3
-    near = jnp.dot(hidden, down[:, :cut], preferred_element_type=jnp.float32).astype(jnp.bfloat16)
-    far = jnp.dot(hidden, down[:, cut:], preferred_element_type=jnp.float32).astype(jnp.bfloat16)
-    mixed = jnp.concatenate(
-        [
-            xor_scatter(stacked(near), "dp", near_first),
-            xor_scatter(stacked(far), "dp", far_first),
-        ],
-        axis=-1,
-    )
+    parts = jnp.dot(hidden, down, preferred_element_type=jnp.float32).astype(jnp.bfloat16)
+    mixed = sum_over_dp(parts.reshape(n_dp, length, D))
 
     own_seed = noise_seeds[:, None]
     tokens = lax.broadcasted_iota(jnp.int32, (length, D), 0) + mp * length
@@ -171,13 +410,8 @@
     gap = flip_sign * (own_pred - partner.astype(jnp.float32))
     gap = xor_scatter(gap.reshape((2,) * len(mp_bits) + (length, D)), "mp", mp_bits)
     gap = gap.astype(jnp.bfloat16)
-    gap_all = jnp.concatenate(
-        [
-            xor_gather(gap[:, :cut], "dp", near_first[::-1]).reshape(n_dp * length, cut),
-            xor_gather(gap[:, cut:], "dp", far_first[::-1]).reshape(n_dp * length, D - cut),
-        ],
-        axis=1,
-    )
+    gap, latents = lax.optimization_barrier((gap, latents))
+    gap_all = gather_over_dp(gap).reshape(n_dp * length, D)
     score_gap = tokens_to_features(gap, "mp")
 
     def over_batch(value):
@@ -186,10 +420,12 @@
     down_sent = over_batch(
         contract_first(hidden, lax.dynamic_slice_in_dim(gap_all, (1 - group) * half, half, 1))
     ).astype(jnp.bfloat16)
+    gap_all, down_sent = lax.optimization_barrier((gap_all, down_sent))
     down_sent = swap(down_sent, "group", 1)
     down_kept = over_batch(
         contract_first(hidden, lax.dynamic_slice_in_dim(gap_all, group * half, half, 1))
     )
+    gap_all, down_kept = lax.optimization_barrier((gap_all, down_kept))
     grad_down = (down_kept + down_sent.astype(jnp.float32)).astype(jnp.bfloat16)
     grad_down = grad_down.reshape((2,) * len(mp_bits) + (share, half))
     grad_down = xor_scatter(grad_down, "mp", mp_bits).astype(jnp.bfloat16)
@@ -199,6 +435,7 @@
         gap_all, down, (((1,), (1,)), ((), ())), preferred_element_type=jnp.float32
     )
     change = (slope * gelu_slope(before)).astype(jnp.bfloat16)
+    change, score_gap = lax.optimization_barrier((change, score_gap))
     up_sent = over_batch(contract_first(normed[:, half:], change)).astype(jnp.bfloat16)
     up_sent = swap(up_sent, "group", 1)
     up_kept = over_batch(contract_first(normed[:, :half], change))

time: 578 us -> 513 us (0.89)
  waiting for transfers between devices: 363 us -> 123 us
  Pallas kernels: 0 us -> 144 us
  blocking collectives: 0 us -> 60.8 us
  starting transfers between devices: 48.5 us -> 24.5 us
  matrix products: 82 us -> 91.4 us
  other arithmetic: 41.4 us -> 33.6 us
  local copies, waits for them, and re-layouts: 34.8 us -> 28.3 us
    ppermute x29 -> x14, waiting for transfers between devices: 305 us -> 96.8 us  [swap(): lax.ppermute(shard, axis, [(i, i ^ bit) for i in range(lax.axis_size(axis...]
    pallas_call x0 -> x2, Pallas kernels: none -> 144 us  [the longest x1 73.5 us: sum_over_dp(): pl.pallas_call(functools.partial(sum_kernel, line), out_shape=jax.ShapeDt...]
    all_to_all x0 -> x1, blocking collectives: none -> 36 us  [per_device(): up = lax.all_to_all(gen_up, 'dp', split_axis=1, concat_axis=0, tiled=True)]
    all_to_all x1, waiting for transfers between devices: 27.4 us -> 0.01 us  [per_device(): lax.all_to_all(gen_down, 'dp', split_axis=0, concat_axis=1, tiled=True)]
    all_to_all x1, waiting for transfers between devices: 0.01 us -> 25.7 us  [per_device(): lax.all_to_all(grad_up, 'dp', split_axis=0, concat_axis=1, tiled=True)]
    unnamed x0 -> x1, blocking collectives: none -> 24.8 us
    all_to_all x1 -> x0, waiting for transfers between devices: 23.9 us -> none  [per_device(): up = lax.all_to_all(gen_up, 'dp', split_axis=1, concat_axis=0, tiled=True)]
    ppermute x29 -> x14, starting transfers between devices: 27.7 us -> 11.5 us  [swap(): lax.ppermute(shard, axis, [(i, i ^ bit) for i in range(lax.axis_size(axis...]
  transfers between devices with their start and end apart: 33 -> 17, of which waited for: 23 -> 8; matrix products, arithmetic and copies ran while one was open for 13% -> 18% of each run, Pallas kernels for 0% -> 0%
where the time goes in v2:
time: 513 us; the launch traced here: 508 us
  Pallas kernels  144 us (28%)
  waiting for transfers between devices  123 us (24%)
  matrix products  91.4 us (18%)
  blocking collectives  60.8 us (12%)
  other arithmetic  33.6 us (7%)
  local copies, waits for them, and re-layouts  28.3 us (6%)
  starting transfers between devices  24.5 us (5%)
    ppermute x14, waiting for transfers between devices, swap(): lax.ppermute(shard, axis, [(i, i ^ bit) for i in range(lax.axis_size(axis...  96.8 us
    pallas_call x1, Pallas kernels, sum_over_dp(): pl.pallas_call(functools.partial(sum_kernel, line), out_shape=jax.ShapeDt...  73.5 us
    pallas_call x1, Pallas kernels, gather_over_dp(): pl.pallas_call(functools.partial(gather_kernel, line), out_shape=jax.Shap...  70.6 us
    all_to_all x1, blocking collectives, per_device(): up = lax.all_to_all(gen_up, 'dp', split_axis=1, concat_axis=0, tiled=True)  36 us
    all_to_all x1, waiting for transfers between devices, per_device(): lax.all_to_all(grad_up, 'dp', split_axis=0, concat_axis=1, tiled=True)  25.7 us
    unnamed x1, blocking collectives  24.8 us
    dot_general x4, matrix products, contract_first(): lax.dot_general(left, right, (((0,), (0,)), ((), ())), preferred_element_...  21.9 us
    dot_general x1, matrix products, score_forward(): jnp.einsum('bsd,kdh->kbsh', normed, weights_in, preferred_element_type=jn...  18.9 us
  transfers between devices with their start and end apart: 17, of which 8 were waited for; matrix products, arithmetic and copies ran while one was open for 18% of the time, Pallas kernels for 0%

profile of v2, /device:TPU:0, one launch (start us, length us, event | category | flops | bytes accessed | tf_op | source)
XLA Modules:
  0.0 507.9 jit_solution(534688132350220307)
XLA Ops:
  0.6 1.5 copy.84
  2.2 36.0 %all_to_all.67 = bf16[192,8,384]{2,0,1:T(8,128)(2,1)S(1)} all-to-all(bf16[192,8,384]{2,0,1:T(8,128)(2,1)S(1)} %bitcast.118), channel_id=1, replica_groups=mesh['group'=2,'dp'=8,'mp'=2] {'dp'}, dimensions={1} | all-to-all | bytes 2359296 | tf_op jit(solution)/shard_map/all_to_all | solution.py:368
  38.2 1.3 copy.83
  39.5 3.6 all-to-all-start.1
  43.0 1.6 collective-permute-start
  45.9 0.8 dynamic-update-slice
  46.6 24.8 %all-reduce = s32[8]{0:T(128)S(1)} all-reduce(s32[8]{0:T(128)S(1)} %dynamic-update-slice), channel_id=1, replica_groups=mesh['group'=2,'dp'=8,'mp'=2] {'dp'}, use_global_device_ids=true, to_apply=%add | all-reduce | flops 8 | bytes 64
  72.0 0.6 add_remainder_fusion
  73.1 1.9 maximum_bitcast_fusion.2
  75.0 2.6 copy.58
  77.7 1.5 collective-permute-start.2
  79.2 8.7 %fusion.21 = f32[8,128]{1,0:T(8,128)S(1)} fusion(s32[3072]{0:T(1024)S(1)} %get-tuple-element.40, s32[3072]{0:T(1024)} %get-tuple-element.41, s32[128]{0:T(128)} %add_multiply_fusion, s32[8]{0:T(128)} %broadcast_multiply_fusion, pred[3072]{0:T(1024)(128)(4,1)S(1)} %fusion.94), kind=kLoop, calls=%fused_computation.27 | loop fusion | flops 66059264 | bytes 32288 | tf_op jit(solution)/shard_map/reduce_sum | solution.py:320
  88.6 0.6 broadcast_add_fusion
  89.8 0.7 add_bitcast_fusion
  90.5 0.6 multiply_bitcast_fusion
  91.1 15.1 %collective-permute-done.2 = bf16[1,384,1536]{1,2,0:T(8,128)(2,1)} collective-permute-done((bf16[1,384,1536]{1,2,0:T(8,128)(2,1)S(1)}, bf16[1,384,1536]{1,2,0:T(8,128)(2,1)}, u32[]{:S(2)}, u32[]{:S(2)}) %collective-permute-start.2) | collective-permute-done | bytes 1179680 | tf_op jit(solution)/shard_map/ppermute | solution.py:22
  106.1 1.5 pad_maximum_fusion
  107.7 2.8 copy.60
  110.6 14.6 %fusion.28 = f32[1024,768]{1,0:T(8,128)} fusion(bf16[1536,768]{0,1:T(8,128)(2,1)} %collective-permute-done.1, bf16[1536,768]{0,1:T(8,128)(2,1)} %bitcast.128, f32[1024]{0:T(1024)S(1)} %copy-done.14, s32[3072]{0:T(1024)S(1)} %get-tuple-element.40, s32[3072]{0:T(1024)S(1)} %copy-done.11, s32[1024]{0:T(1024)S(1)} %add_bitcast_fusion, ...), kind=kOutput, calls=%fused_computation.40 | convolution fusion | flops 4901044224 | bytes 7900160 | tf_op jit(solution)/shard_map/dot_general | solution.py:389
  125.2 9.1 %convolution_convert_fusion = bf16[1024,3072]{1,0:T(8,128)(2,1)S(1)} fusion(bf16[768,1536]{1,0:T(8,128)(2,1)S(1)} %collective-permute-done.3, bf16[768,1536]{1,0:T(8,128)(2,1)S(1)} %bitcast.125, pred[]{:T(512)S(6)} %eq.5, f32[1024,768]{1,0:T(8,128)} %fusion.28), kind=kOutput, calls=%fused_computation.35 | convolution fusion | flops 4863295488 | bytes 14155777 | tf_op jit(solution)/shard_map/dot_general | solution.py:392
  134.4 73.5 %shard_map.93 = f32[128,3072]{1,0:T(8,128)S(1)} custom-call(bf16[8,128,3072]{2,1,0:T(8,128)(2,1)S(1)} %bitcast.103), custom_call_target="tpu_custom_call" | custom-call | flops 6291456 | bytes 125829120 | tf_op jit(solution)/shard_map/pallas_call | solution.py:216
  207.9 3.0 fusion.61
  211.2 1.6 collective-permute-start.4
  212.8 15.6 %collective-permute-done.4 = bf16[1,128,3072]{2,1,0:T(8,128)(2,1)S(1)} collective-permute-done((bf16[1,128,3072]{2,1,0:T(8,128)(2,1)S(1)}, bf16[1,128,3072]{2,1,0:T(8,128)(2,1)S(1)}, u32[]{:S(2)}, u32[]{:S(2)}) %collective-permute-start.4) | collective-permute-done | bytes 786464 | tf_op jit(solution)/shard_map/ppermute | solution.py:22
  228.6 3.4 collective-permute-done.5
  232.0 18.9 %convert_bitcast_fusion = bf16[3,2,256,1536]{3,2,0,1:T(8,128)(2,1)S(1)} fusion(bf16[1,3,3072,1536]{3,2,1,0:T(8,128)(2,1)} %param.10, bf16[1,256,3072]{2,1,0:T(8,128)(2,1)S(1)} %bitcast.139, bf16[1,256,3072]{2,1,0:T(8,128)(2,1)S(1)} %bitcast.132), kind=kOutput, calls=%fused_computation.49 | convolution fusion | flops 14504165376 | bytes 36175872 | tf_op jit(solution)/shard_map/bsd,kdh->kbsh/dot_general | solution.py:334
  250.9 1.5 fusion.108
  252.4 1.6 copy.61
  254.0 1.7 copy.62
  255.7 1.6 copy.63
  257.2 2.9 fusion.27
  260.2 1.3 fusion.87
  261.5 1.0 fusion.109
  262.6 3.8 fusion.34
  266.7 1.6 collective-permute-start.8
  268.3 1.7 collective-permute-done.6
  270.1 1.2 copy-done.6
  271.2 7.1 %subtract_multiply_fusion = f32[256,3072]{1,0:T(8,128)S(1)} fusion(bf16[256,3072]{1,0:T(8,128)(2,1)} %copy-done.6, f32[]{:T(128)S(6)} %convert_element_type.127, bf16[256,1536]{0,1:T(8,128)(2,1)} %bitcast.123, bf16[1,1536,3072]{2,1,0:T(8,128)(2,1)} %param.11), kind=kOutput, calls=%fused_computation.74 | convolution fusion | flops 2418278400 | bytes 14942212 | tf_op jit(solution)/shard_map/dot_general | solution.py:351
  278.4 1.0 fusion.89
  279.3 1.5 collective-permute-start.7
  280.9 9.3 %fusion.22 = bf16[1024,3072]{1,0:T(8,128)(2,1)} fusion(f32[1024]{0:T(1024)S(1)} %copy-done.15, s32[3072]{0:T(1024)S(1)} %get-tuple-element.40, s32[3072]{0:T(1024)S(1)} %copy-done.12, s32[1024]{0:T(1024)S(1)} %add_bitcast_fusion, pred[3072]{0:T(1024)(128)(4,1)S(1)} %copy-done.18), kind=kLoop, calls=%fused_computation.28 | loop fusion | flops 59768832 | bytes 6327296 | tf_op jit(solution)/shard_map/convert_element_type | solution.py:387
  290.2 1.8 constant_dynamic-update-slice_fusion
  291.9 7.3 %collective-permute-done.7 = bf16[1,128,3072]{2,1,0:T(8,128)(2,1)} collective-permute-done((bf16[1,128,3072]{2,1,0:T(8,128)(2,1)}, bf16[1,128,3072]{2,1,0:T(8,128)(2,1)}, u32[]{:S(2)}, u32[]{:S(2)}) %collective-permute-start.7) | collective-permute-done | bytes 786464 | tf_op jit(solution)/shard_map/ppermute | solution.py:22
  299.2 2.2 fusion.88.own
  301.4 70.6 %shard_map.94 = bf16[8,128,3072]{2,1,0:T(8,128)(2,1)} custom-call(bf16[128,3072]{1,0:T(8,128)(2,1)} %fusion.88.own), custom_call_target="tpu_custom_call" | custom-call | bytes 125829120 | tf_op jit(solution)/shard_map/pallas_call | solution.py:300
  372.0 6.1 %multiply_convert_fusion.1 = bf16[768,1536]{1,0:T(8,128)(2,1)} fusion(bf16[1024,3072]{1,0:T(8,128)(2,1)} %bitcast.110, s32[]{:T(128)S(6)} %select_n.48, f32[1024,768]{1,0:T(8,128)S(1)} %copy-done.23), kind=kOutput, calls=%fused_computation.48 | convolution fusion | flops 2425356288 | bytes 8650756 | tf_op jit(solution)/shard_map/dot_general | solution.py:357
  378.1 2.9 convolution_multiply_fusion
  381.2 1.5 collective-permute-start.9
  382.7 11.7 %fusion.51 = bf16[1024,768]{1,0:T(8,128)(2,1)} fusion(f32[1024,768]{1,0:T(8,128)} %fusion.28, bf16[1024,3072]{1,0:T(8,128)(2,1)S(1)} %bitcast.112, bf16[768,1536]{1,0:T(8,128)(2,1)} %copy-done.21, bf16[768,1536]{1,0:T(8,128)(2,1)S(1)} %bitcast.126, pred[]{:T(512)S(6)} %eq.5), kind=kOutput, calls=%fused_computation.66 | convolution fusion | flops 4868014080 | bytes 15728641 | tf_op jit(solution)/shard_map/dot_general | solution.py:434
  394.5 5.7 %multiply_convert_fusion = bf16[1536,768]{0,1:T(8,128)(2,1)} fusion(bf16[1024,768]{1,0:T(8,128)(2,1)} %fusion.51, bf16[1024,3072]{1,0:T(8,128)(2,1)S(1)} %bitcast.109), kind=kOutput, calls=%fused_computation.47 | convolution fusion | flops 2418278400 | bytes 7077888 | tf_op jit(solution)/shard_map/dot_general | solution.py:357
  400.7 0.8 add_convert_fusion
  401.6 0.6 collective-permute-start.13
  402.2 27.3 %collective-permute-done.13 = bf16[1,384,1536]{2,1,0:T(8,128)(2,1)S(1)} collective-permute-done((bf16[1,384,1536]{2,1,0:T(8,128)(2,1)S(1)}, bf16[1,384,1536]{2,1,0:T(8,128)(2,1)S(1)}, u32[]{:S(2)}, u32[]{:S(2)}) %collective-permute-start.13) | collective-permute-done | bytes 1179680 | tf_op jit(solution)/shard_map/ppermute | solution.py:22
  429.8 1.4 copy.70
  431.2 3.8 all-to-all-start.3
  435.0 7.3 %add_convert_fusion.1 = bf16[1536,768]{0,1:T(8,128)(2,1)} fusion(bf16[1536,768]{0,1:T(8,128)(2,1)} %collective-permute-done.10, bf16[1024,768]{1,0:T(8,128)(2,1)} %fusion.51, bf16[1024,3072]{1,0:T(8,128)(2,1)} %fusion.22), kind=kOutput, calls=%fused_computation.46 | convolution fusion | flops 2420637696 | bytes 9437184 | tf_op jit(solution)/shard_map/dot_general | solution.py:357
  442.3 3.0 copy.68
  445.4 0.6 collective-permute-start.11
  446.1 26.4 %collective-permute-done.11 = bf16[1,1536,384]{2,1,0:T(8,128)(2,1)S(1)} collective-permute-done((bf16[1,1536,384]{2,1,0:T(8,128)(2,1)S(1)}, bf16[1,1536,384]{2,1,0:T(8,128)(2,1)S(1)}, u32[]{:S(2)}, u32[]{:S(2)}) %collective-permute-start.11) | collective-permute-done | bytes 1179680 | tf_op jit(solution)/shard_map/ppermute | solution.py:22
  472.5 1.3 add_convert_fusion.2
  473.8 5.7 %all-to-all-start.2 = ((bf16[8,192,384]{2,1,0:T(8,128)(2,1)}), bf16[8,192,384]{2,1,0:T(8,128)(2,1)S(1)}, u32[]{:S(2)}, u32[]{:S(2)}) async-start(bf16[8,192,384]{2,1,0:T(8,128)(2,1)} %bitcast.41), calls=%async_computation.2 | async-start | bytes 2359296 | tf_op jit(solution)/shard_map/all_to_all | solution.py:446
  479.5 1.2 copy.80
  480.7 25.7 %all-to-all-done.2 = bf16[8,192,384]{2,1,0:T(8,128)(2,1)S(1)} async-done(((bf16[8,192,384]{2,1,0:T(8,128)(2,1)}), bf16[8,192,384]{2,1,0:T(8,128)(2,1)S(1)}, u32[]{:S(2)}, u32[]{:S(2)}) %all-to-all-start.2) | async-done | bytes 1179680 | tf_op jit(solution)/shard_map/all_to_all | solution.py:446
  506.4 1.2 copy.79
  (91 shorter events, 4.4 us)
Async XLA Ops:
  0.6 37.5 %copy-start.8 = (bf16[3072,192]{0,1:T(8,128)(2,1)S(1)}, bf16[3072,192]{0,1:T(8,128)(2,1)}, u32[]{:S(2)}) copy-start(bf16[3072,192]{0,1:T(8,128)(2,1)} %param.9) | copy-start | bytes 3538948
  2.1 43.1 %copy-start.22 = (u32[32]{0:T(128)S(1)}, u32[32]{0:T(128)}, u32[]{:S(2)}) copy-start(u32[32]{0:T(128)} %constant.129) | copy-start | bytes 388
  38.1 35.0 %copy-start.2 = (bf16[192,8,384]{2,0,1:T(8,128)(2,1)}, bf16[192,8,384]{2,0,1:T(8,128)(2,1)S(1)}, u32[]{:S(2)}) copy-start(bf16[192,8,384]{2,0,1:T(8,128)(2,1)S(1)} %all_to_all.67) | copy-start | bytes 3538948
  39.5 38.2 %all-to-all-start.1 = ((bf16[8,384,192]{1,2,0:T(8,128)(2,1)}), bf16[8,384,192]{1,2,0:T(8,128)(2,1)S(1)}, u32[]{:S(2)}, u32[]{:S(2)}) async-start(bf16[8,384,192]{1,2,0:T(8,128)(2,1)} %bitcast.101), calls=%async_computation.1 | async-start | bytes 2359296 | tf_op jit(solution)/shard_map/all_to_all | solution.py:370
  43.0 30.1 %collective-permute-start = (bf16[1,1536,384]{2,1,0:T(8,128)(2,1)S(1)}, bf16[1,1536,384]{2,1,0:T(8,128)(2,1)}, u32[]{:S(2)}, u32[]{:S(2)}) collective-permute-start(bf16[1,1536,384]{2,1,0:T(8,128)(2,1)S(1)} %bitcast.121), channel_id=1, source_target_pairs={{0,1},{1,0},{2,3},{3,2},{4,5},{5,4},{6,7},{7,6},{8,9},{9,8},{10,11... | collective-permute-start | bytes 3538952 | tf_op jit(solution)/shard_map/ppermute | solution.py:22
  72.0 7.2 %copy-start.16 = (pred[3072]{0:T(1024)(128)(4,1)}, pred[3072]{0:T(1024)(128)(4,1)S(1)}, u32[]{:S(2)}) copy-start(pred[3072]{0:T(1024)(128)(4,1)S(1)} %fusion.94) | copy-start | bytes 9220
  77.7 33.0 %collective-permute-start.1 = (bf16[1536,768]{0,1:T(8,128)(2,1)}, bf16[1536,768]{0,1:T(8,128)(2,1)}, u32[]{:S(2)}, u32[]{:S(2)}) collective-permute-start(bf16[1536,768]{0,1:T(8,128)(2,1)} %bitcast.127), channel_id=1, source_target_pairs={{0,16},{16,0},{1,17},{17,1},{2,18},{18,2},{3,19},{19,3},{4,20},{20... | collective-permute-start | bytes 7077896 | tf_op jit(solution)/shard_map/ppermute | solution.py:22
  77.7 28.5 %collective-permute-start.2 = (bf16[1,384,1536]{1,2,0:T(8,128)(2,1)S(1)}, bf16[1,384,1536]{1,2,0:T(8,128)(2,1)}, u32[]{:S(2)}, u32[]{:S(2)}) collective-permute-start(bf16[1,384,1536]{1,2,0:T(8,128)(2,1)S(1)} %bitcast.119), channel_id=1, source_target_pairs={{0,1},{1,0},{2,3},{3,2},{4,5},{5,4},{6,7},{7,6},{8,9},{9,8},{10,11... | collective-permute-start | bytes 3538952 | tf_op jit(solution)/shard_map/ppermute | solution.py:22
  107.7 2.9 copy-start.11
  107.7 2.9 copy-start.14
  107.7 2.9 copy-start.17
  110.5 14.7 %copy-start.4 = (bf16[2,384,1536]{2,1,0:T(8,128)(2,1)S(1)}, bf16[2,384,1536]{2,1,0:T(8,128)(2,1)}, u32[]{:S(2)}) copy-start(bf16[2,384,1536]{2,1,0:T(8,128)(2,1)} %copy.60) | copy-start | bytes 7077892
  110.5 14.7 %collective-permute-start.3 = (bf16[768,1536]{1,0:T(8,128)(2,1)}, bf16[768,1536]{1,0:T(8,128)(2,1)S(1)}, u32[]{:S(2)}, u32[]{:S(2)}) collective-permute-start(bf16[768,1536]{1,0:T(8,128)(2,1)} %bitcast.124), channel_id=1, source_target_pairs={{0,16},{16,0},{1,17},{17,1},{2,18},{18,2},{3,19},{19,3},{4,20},{20... | collective-permute-start | bytes 7077896 | tf_op jit(solution)/shard_map/ppermute | solution.py:22
  125.2 9.2 %copy-start.21 = (bf16[768,1536]{1,0:T(8,128)(2,1)}, bf16[768,1536]{1,0:T(8,128)(2,1)S(1)}, u32[]{:S(2)}) copy-start(bf16[768,1536]{1,0:T(8,128)(2,1)S(1)} %collective-permute-done.3) | copy-start | bytes 7077892
  134.4 73.5 %copy-start.13 = (s32[3072]{0:T(1024)S(1)}, s32[3072]{0:T(1024)}, u32[]{:S(2)}) copy-start(s32[3072]{0:T(1024)} %iota_multiply_fusion) | copy-start | bytes 36868
  134.4 73.5 %copy-start.19 = (s32[128]{0:T(128)S(1)}, s32[128]{0:T(128)}, u32[]{:S(2)}) copy-start(s32[128]{0:T(128)} %get-tuple-element.38) | copy-start | bytes 1540
  134.4 73.5 %copy-start.20 = (s32[128]{0:T(128)S(1)}, s32[128]{0:T(128)}, u32[]{:S(2)}) copy-start(s32[128]{0:T(128)} %get-tuple-element.39) | copy-start | bytes 1540
  211.2 17.2 %collective-permute-start.4 = (bf16[1,128,3072]{2,1,0:T(8,128)(2,1)S(1)}, bf16[1,128,3072]{2,1,0:T(8,128)(2,1)S(1)}, u32[]{:S(2)}, u32[]{:S(2)}) collective-permute-start(bf16[1,128,3072]{2,1,0:T(8,128)(2,1)S(1)} %fusion.90), channel_id=1, source_target_pairs={{0,1},{1,0},{2,3},{3,2},{4,5},{5,4},{6,7},{7,6},{8,9},{9,8},{10,11... | collective-permute-start | bytes 2359304 | tf_op jit(solution)/shard_map/ppermute | solution.py:22
  228.5 3.5 collective-permute-start.5
  257.2 2.9 copy-start.7
  257.2 5.3 %slice-start = ((s8[9437184]{0:T(1024)(128)(4,1)}), s8[4194304]{0:T(1024)(128)(4,1)S(1)}, s32[]{:S(2)}) async-start(s8[9437184]{0:T(1024)(128)(4,1)} %bitcast.104), calls=%async_computation.4 | async-start | bytes 8388608
  260.1 2.4 slice-start.1
  260.1 2.5 slice-start.2
  262.6 4.0 copy-start.3
  266.4 3.6 collective-permute-start.6
  266.7 3.4 copy-start.10
  266.7 23.4 %collective-permute-start.8 = (bf16[128,1536]{1,0:T(8,128)(2,1)S(1)}, bf16[128,1536]{1,0:T(8,128)(2,1)}, u32[]{:S(2)}, u32[]{:S(2)}) collective-permute-start(bf16[128,1536]{1,0:T(8,128)(2,1)S(1)} %get-tuple-element.34), channel_id=1, source_target_pairs={{0,1},{1,0},{2,3},{3,2},{4,5},{5,4},{6,7},{7,6},{8,9},{9,8},{10,11... | collective-permute-start | bytes 1179656 | tf_op jit(solution)/shard_map/ppermute | solution.py:22
  270.1 1.2 copy-start.6
  271.2 9.6 %copy-start.12 = (s32[3072]{0:T(1024)S(1)}, s32[3072]{0:T(1024)}, u32[]{:S(2)}) copy-start(s32[3072]{0:T(1024)} %get-tuple-element.41) | copy-start | bytes 36868
  271.2 9.6 %copy-start.15 = (f32[1024]{0:T(1024)S(1)}, f32[1024]{0:T(1024)}, u32[]{:S(2)}) copy-start(f32[1024]{0:T(1024)} %multiply_bitcast_fusion) | copy-start | bytes 12292
  271.2 9.6 %copy-start.18 = (pred[3072]{0:T(1024)(128)(4,1)S(1)}, pred[3072]{0:T(1024)(128)(4,1)}, u32[]{:S(2)}) copy-start(pred[3072]{0:T(1024)(128)(4,1)} %copy-done.16) | copy-start | bytes 9220
  279.3 19.9 %collective-permute-start.7 = (bf16[1,128,3072]{2,1,0:T(8,128)(2,1)}, bf16[1,128,3072]{2,1,0:T(8,128)(2,1)}, u32[]{:S(2)}, u32[]{:S(2)}) collective-permute-start(bf16[1,128,3072]{2,1,0:T(8,128)(2,1)} %fusion.89), channel_id=1, source_target_pairs={{0,1},{1,0},{2,3},{3,2},{4,5},{5,4},{6,7},{7,6},{8,9},{9,8},{10,11... | collective-permute-start | bytes 2359304 | tf_op jit(solution)/shard_map/ppermute | solution.py:22
  301.4 70.6 %copy-start.23 = (f32[1024,768]{1,0:T(8,128)S(1)}, f32[1024,768]{1,0:T(8,128)}, u32[]{:S(2)}) copy-start(f32[1024,768]{1,0:T(8,128)} %fusion.28) | copy-start | bytes 9437188
  372.0 6.1 %copy-start.1 = (bf16[8,128,3072]{2,1,0:T(8,128)(2,1)S(1)}, bf16[8,128,3072]{2,1,0:T(8,128)(2,1)}, u32[]{:S(2)}) copy-start(bf16[8,128,3072]{2,1,0:T(8,128)(2,1)} %shard_map.94) | copy-start | bytes 18874372
  378.1 3.0 copy-start
  378.1 4.6 copy-start.5
  381.2 13.3 %slice-start.3 = ((s8[6291456]{0:T(1024)(128)(4,1)}), s8[4194304]{0:T(1024)(128)(4,1)S(1)}, s32[]{:S(2)}) async-start(s8[6291456]{0:T(1024)(128)(4,1)} %bitcast.108), calls=%async_computation.7 | async-start | bytes 8388608
  381.2 13.3 %slice-start.4 = ((s8[6291456]{0:T(1024)(128)(4,1)}), s8[2097152]{0:T(1024)(128)(4,1)S(1)}, s32[]{:S(2)}) async-start(s8[6291456]{0:T(1024)(128)(4,1)} %bitcast.108), calls=%async_computation.8 | async-start | bytes 4194304
  381.2 13.2 %collective-permute-start.9 = (bf16[128,1536]{1,0:T(8,128)(2,1)S(1)}, bf16[128,1536]{1,0:T(8,128)(2,1)S(1)}, u32[]{:S(2)}, u32[]{:S(2)}) collective-permute-start(bf16[128,1536]{1,0:T(8,128)(2,1)S(1)} %get-tuple-element.32), channel_id=1, source_target_pairs={{0,1},{1,0},{2,3},{3,2},{4,5},{5,4},{6,7},{7,6},{8,9},{9,8},{10,11... | collective-permute-start | bytes 1179656 | tf_op jit(solution)/shard_map/ppermute | solution.py:22
  382.7 18.0 %collective-permute-start.12 = (bf16[768,1536]{1,0:T(8,128)(2,1)}, bf16[768,1536]{1,0:T(8,128)(2,1)S(1)}, u32[]{:S(2)}, u32[]{:S(2)}) collective-permute-start(bf16[768,1536]{1,0:T(8,128)(2,1)} %multiply_convert_fusion.1), channel_id=1, source_target_pairs={{0,16},{16,0},{1,17},{17,1},{2,18},{18,2},{3,19},{19,3},{4,20},{20... | collective-permute-start | bytes 7077896 | tf_op jit(solution)/shard_map/ppermute | solution.py:22
  394.5 5.7 %copy-start.9 = (bf16[256,1536]{1,0:T(8,128)(2,1)}, bf16[256,1536]{1,0:T(8,128)(2,1)S(1)}, u32[]{:S(2)}) copy-start(bf16[256,1536]{1,0:T(8,128)(2,1)S(1)} %constant_dynamic-update-slice_fusion.1) | copy-start | bytes 2359300
  400.2 34.8 %collective-permute-start.10 = (bf16[1536,768]{0,1:T(8,128)(2,1)}, bf16[1536,768]{0,1:T(8,128)(2,1)}, u32[]{:S(2)}, u32[]{:S(2)}) collective-permute-start(bf16[1536,768]{0,1:T(8,128)(2,1)} %multiply_convert_fusion), channel_id=1, source_target_pairs={{0,16},{16,0},{1,17},{17,1},{2,18},{18,2},{3,19},{19,3},{4,20},{20... | collective-permute-start | bytes 7077896 | tf_op jit(solution)/shard_map/ppermute | solution.py:22
  401.6 27.9 %collective-permute-start.13 = (bf16[1,384,1536]{2,1,0:T(8,128)(2,1)S(1)}, bf16[1,384,1536]{2,1,0:T(8,128)(2,1)S(1)}, u32[]{:S(2)}, u32[]{:S(2)}) collective-permute-start(bf16[1,384,1536]{2,1,0:T(8,128)(2,1)S(1)} %slice_bitcast_fusion.1), channel_id=1, source_target_pairs={{0,1},{1,0},{2,3},{3,2},{4,5},{5,4},{6,7},{7,6},{8,9},{9,8},{10,11... | collective-permute-start | bytes 3538952 | tf_op jit(solution)/shard_map/ppermute | solution.py:22
  431.2 42.6 %all-to-all-start.3 = ((bf16[384,8,192]{0,2,1:T(8,128)(2,1)}), bf16[384,8,192]{0,2,1:T(8,128)(2,1)S(1)}, u32[]{:S(2)}, u32[]{:S(2)}) async-start(bf16[384,8,192]{0,2,1:T(8,128)(2,1)} %bitcast.45), calls=%async_computation.3 | async-start | bytes 2359296 | tf_op jit(solution)/shard_map/all_to_all | solution.py:432
  445.4 27.1 %collective-permute-start.11 = (bf16[1,1536,384]{2,1,0:T(8,128)(2,1)S(1)}, bf16[1,1536,384]{2,1,0:T(8,128)(2,1)S(1)}, u32[]{:S(2)}, u32[]{:S(2)}) collective-permute-start(bf16[1,1536,384]{2,1,0:T(8,128)(2,1)S(1)} %slice.75), channel_id=1, source_target_pairs={{0,1},{1,0},{2,3},{3,2},{4,5},{5,4},{6,7},{7,6},{8,9},{9,8},{10,11... | collective-permute-start | bytes 3538952 | tf_op jit(solution)/shard_map/ppermute | solution.py:22
  473.8 32.6 %all-to-all-start.2 = ((bf16[8,192,384]{2,1,0:T(8,128)(2,1)}), bf16[8,192,384]{2,1,0:T(8,128)(2,1)S(1)}, u32[]{:S(2)}, u32[]{:S(2)}) async-start(bf16[8,192,384]{2,1,0:T(8,128)(2,1)} %bitcast.41), calls=%async_computation.2 | async-start | bytes 2359296 | tf_op jit(solution)/shard_map/all_to_all | solution.py:446

commit v3 on v2

--- a/solution.py
+++ b/solution.py
@@ -34,14 +34,18 @@
     return out
 
 
-def xor_scatter(parts, axis, order):
+def xor_scatter(parts, axis, order, beside=None):
     bits = bits_of(axis)
     for bit in order:
         at = bits.index(bit)
         kept = lax.slice_in_dim(parts, 0, 1, axis=at)
         sent = lax.slice_in_dim(parts, 1, 2, axis=at).astype(jnp.bfloat16)
-        parts = kept.astype(jnp.float32) + swap(sent, axis, bit).astype(jnp.float32)
-    return parts.reshape(parts.shape[len(bits):])
+        came = swap(sent, axis, bit)
+        if beside is not None and bit == order[0]:
+            came, beside = lax.optimization_barrier((came, beside))
+        parts = kept.astype(jnp.float32) + came.astype(jnp.float32)
+    parts = parts.reshape(parts.shape[len(bits):])
+    return parts if beside is None else (parts, beside)
 
 
 def tokens_to_features(shard, axis):
@@ -328,12 +332,15 @@
     )
 
 
-def score_forward(normed, weights_in, weights_out):
-    pairs, length = normed.shape[:2]
-    local_heads = weights_in.shape[2] // HEAD_DIM
-    projected = jnp.einsum(
+def project(normed, weights_in):
+    return jnp.einsum(
         "bsd,kdh->kbsh", normed, weights_in, preferred_element_type=jnp.float32
     ).astype(jnp.bfloat16)
+
+
+def attend(projected):
+    pairs, length, width = projected[0].shape
+    local_heads = width // HEAD_DIM
     shape = (pairs, length, local_heads, HEAD_DIM)
     query = projected[0].reshape(shape)
     keys = projected[1].reshape(shape)
@@ -346,11 +353,7 @@
     attended = jnp.einsum(
         "bhqk,bkhe->bqhe", probs, values, preferred_element_type=jnp.float32
     ).astype(jnp.bfloat16)
-    attended = attended.reshape(pairs, length, local_heads * HEAD_DIM)
-    return [
-        jnp.dot(attended[pair], weights_out, preferred_element_type=jnp.float32)
-        for pair in (1, 0)
-    ]
+    return attended.reshape(pairs, length, width)
 
 
 def contract_first(left, right):
@@ -380,7 +383,12 @@
         jnp.concatenate([down_other, down], axis=1),
     )
 
-    seeds = lax.all_gather(noise_seeds, "dp", tiled=True)[:, None, None]
+    seeds = xor_gather(noise_seeds, "dp", bits_of("dp")[::-1])
+    seeds = seeds.transpose(tuple(range(seeds.ndim))[::-1]).reshape(1, n_dp)
+    index = lax.broadcasted_iota(jnp.int32, (n_dp, n_dp), 0)
+    column = lax.broadcasted_iota(jnp.int32, (n_dp, n_dp), 1)
+    seeds = jnp.sum(jnp.where(index ^ lax.axis_index("dp") == column, seeds, 0), axis=1)
+    seeds = seeds[:, None, None]
     shape = (n_dp, length, D)
     tokens = lax.broadcasted_iota(jnp.int32, shape, 1) + mp * length
     feature = (lax.broadcasted_iota(jnp.int32, shape, 2) + group * half) % D
@@ -402,14 +410,37 @@
     score_normed = rms_norm(noisy.astype(jnp.float32)).astype(jnp.bfloat16)
 
     sample = xor_gather(score_normed, "mp", mp_bits).reshape(SEQ, D)
-    paired = jnp.stack([sample, swap(sample, "group", 1)])
+    near = jnp.stack([score_normed, swap(score_normed, "group", 1)])
+    near = project(near, score_qkv[0])
+    sample, near = lax.optimization_barrier((sample[length:], near))
+    far = project(jnp.stack([sample, swap(sample, "group", 1)]), score_qkv[0])
     latents = tokens_to_features(latent, "mp")
-    other_pred, own_pred = score_forward(paired, score_qkv[0], score_out[0])
-    partner = swap(other_pred.astype(jnp.bfloat16), "group", 1)
+    attended = attend([jnp.concatenate([near[k], far[k]], axis=1) for k in range(3)])
+
+    def predict(pair, start, stop):
+        return jnp.dot(
+            attended[pair, start:stop], score_out[0], preferred_element_type=jnp.float32
+        )
+
     flip_sign = (2 * group - 1).astype(jnp.float32)
-    gap = flip_sign * (own_pred - partner.astype(jnp.float32))
-    gap = xor_scatter(gap.reshape((2,) * len(mp_bits) + (length, D)), "mp", mp_bits)
-    gap = gap.astype(jnp.bfloat16)
+    split = SEQ // 2
+    sent = [
+        predict(1, start, start + split).astype(jnp.bfloat16) for start in (split, 0)
+    ]
+    came = [swap(part, "group", 1) for part in sent]
+    gap = [
+        flip_sign * (predict(0, start, start + split) - part.astype(jnp.float32))
+        for start, part in zip((split, 0), came)
+    ]
+    gap = [part.astype(jnp.bfloat16) for part in gap]
+    blocks = (1,) + (2,) * (len(mp_bits) - 1) + (length, D)
+    came = swap(gap[0].reshape(blocks), "mp", mp_bits[0])
+    gap = gap[1].reshape(blocks).astype(jnp.float32) + came.astype(jnp.float32)
+    for at, bit in enumerate(mp_bits[1:], 1):
+        kept = lax.slice_in_dim(gap, 0, 1, axis=at)
+        came = swap(lax.slice_in_dim(gap, 1, 2, axis=at).astype(jnp.bfloat16), "mp", bit)
+        gap = kept + came.astype(jnp.float32)
+    gap = gap.reshape(length, D).astype(jnp.bfloat16)
     gap, latents = lax.optimization_barrier((gap, latents))
     gap_all = gather_over_dp(gap).reshape(n_dp * length, D)
     score_gap = tokens_to_features(gap, "mp")
@@ -428,20 +459,21 @@
     gap_all, down_kept = lax.optimization_barrier((gap_all, down_kept))
     grad_down = (down_kept + down_sent.astype(jnp.float32)).astype(jnp.bfloat16)
     grad_down = grad_down.reshape((2,) * len(mp_bits) + (share, half))
-    grad_down = xor_scatter(grad_down, "mp", mp_bits).astype(jnp.bfloat16)
-    grad_down = lax.all_to_all(grad_down, "dp", split_axis=1, concat_axis=0, tiled=True)
 
     slope = lax.dot_general(
         gap_all, down, (((1,), (1,)), ((), ())), preferred_element_type=jnp.float32
     )
     change = (slope * gelu_slope(before)).astype(jnp.bfloat16)
-    change, score_gap = lax.optimization_barrier((change, score_gap))
+    change, score_gap, grad_down = lax.optimization_barrier((change, score_gap, grad_down))
     up_sent = over_batch(contract_first(normed[:, half:], change)).astype(jnp.bfloat16)
     up_sent = swap(up_sent, "group", 1)
     up_kept = over_batch(contract_first(normed[:, :half], change))
     grad_up = (up_kept + up_sent.astype(jnp.float32)).astype(jnp.bfloat16)
     grad_up = jnp.moveaxis(grad_up.reshape(half, n_mp, share), 1, 0)
     grad_up = grad_up.reshape((2,) * len(mp_bits) + (half, share))
+    grad_down, grad_up = xor_scatter(grad_down, "mp", mp_bits, grad_up)
+    grad_down = grad_down.astype(jnp.bfloat16)
+    grad_down = lax.all_to_all(grad_down, "dp", split_axis=1, concat_axis=0, tiled=True)
     grad_up = xor_scatter(grad_up, "mp", mp_bits).astype(jnp.bfloat16)
     grad_up = lax.all_to_all(grad_up, "dp", split_axis=0, concat_axis=1, tiled=True)
     return (latents[None], score_gap[None], grad_up, grad_down)

time: 513 us -> 512 us (level)
  blocking collectives: 60.8 us -> 36 us
  waiting for transfers between devices: 123 us -> 139 us
    unnamed x1 -> x0, blocking collectives: 24.8 us -> none
    ppermute x14 -> x19, waiting for transfers between devices: 96.8 us -> 114 us  [swap(): lax.ppermute(shard, axis, [(i, i ^ bit) for i in range(lax.axis_size(axis...]
    ppermute x14 -> x19, starting transfers between devices: 11.5 us -> 14.9 us  [swap(): lax.ppermute(shard, axis, [(i, i ^ bit) for i in range(lax.axis_size(axis...]
    dot_general x5 -> x8, matrix products: 34.1 us -> 36.1 us  [the longest x2 26.4 us: project(): jnp.einsum('bsd,kdh->kbsh', normed, weights_in, preferred_element_type=jn...]
  transfers between devices with their start and end apart: 17 -> 22, of which waited for: 8 -> 11; matrix products, arithmetic and copies ran while one was open for 18% -> 19% of each run, Pallas kernels for 0% -> 0%
where the time goes in v3:
time: 512 us; the launch traced here: 507 us
  Pallas kernels  144 us (28%)
  waiting for transfers between devices  139 us (27%)
  matrix products  92.1 us (18%)
  other arithmetic  37.1 us (7%)
  blocking collectives  36 us (7%)
  local copies, waits for them, and re-layouts  28 us (5%)
  starting transfers between devices  27.7 us (5%)
    ppermute x19, waiting for transfers between devices, swap(): lax.ppermute(shard, axis, [(i, i ^ bit) for i in range(lax.axis_size(axis...  114 us
    pallas_call x1, Pallas kernels, sum_over_dp(): pl.pallas_call(functools.partial(sum_kernel, line), out_shape=jax.ShapeDt...  73.5 us
    pallas_call x1, Pallas kernels, gather_over_dp(): pl.pallas_call(functools.partial(gather_kernel, line), out_shape=jax.Shap...  70.3 us
    all_to_all x1, blocking collectives, per_device(): up = lax.all_to_all(gen_up, 'dp', split_axis=1, concat_axis=0, tiled=True)  36 us
    dot_general x2, matrix products, project(): jnp.einsum('bsd,kdh->kbsh', normed, weights_in, preferred_element_type=jn...  26.4 us
    all_to_all x1, waiting for transfers between devices, per_device(): lax.all_to_all(grad_up, 'dp', split_axis=0, concat_axis=1, tiled=True)  25.7 us
    dot_general x4, matrix products, contract_first(): lax.dot_general(left, right, (((0,), (0,)), ((), ())), preferred_element_...  20.5 us
    ppermute x19, starting transfers between devices, swap(): lax.ppermute(shard, axis, [(i, i ^ bit) for i in range(lax.axis_size(axis...  14.9 us
  transfers between devices with their start and end apart: 22, of which 11 were waited for; matrix products, arithmetic and copies ran while one was open for 19% of the time, Pallas kernels for 0%

profile of v3, /device:TPU:0, one launch (start us, length us, event | category | flops | bytes accessed | tf_op | source)
XLA Modules:
  0.0 507.1 jit_solution(725333585563769002)
XLA Ops:
  0.6 1.5 copy.110
  2.1 36.0 %all_to_all.67 = bf16[192,8,384]{2,0,1:T(8,128)(2,1)S(1)} all-to-all(bf16[192,8,384]{2,0,1:T(8,128)(2,1)S(1)} %bitcast.147), channel_id=1, replica_groups=mesh['group'=2,'dp'=8,'mp'=2] {'dp'}, dimensions={1} | all-to-all | bytes 2359296 | tf_op jit(solution)/shard_map/all_to_all | solution.py:371
  38.1 1.3 copy.109
  39.4 3.6 all-to-all-start.1
  43.0 2.8 collective-permute-start
  47.7 1.5 collective-permute-start.3
  51.1 20.3 %collective-permute-done = s32[1,1,1,1]{0,1,2,3:T(1,128)} collective-permute-done((s32[1,1,1,1]{0,1,2,3:T(1,128)}, s32[1,1,1,1]{0,1,2,3:T(1,128)}, u32[]{:S(2)}, u32[]{:S(2)}) %collective-permute-start) | collective-permute-done | bytes 36 | tf_op jit(solution)/shard_map/ppermute | solution.py:22
  72.1 3.6 collective-permute-done.1
  76.3 1.3 collective-permute-start.2
  77.6 2.3 collective-permute-done.2
  79.9 0.7 add_bitcast_fusion.1
  81.5 1.9 maximum_bitcast_fusion
  83.4 2.7 copy.79
  86.1 1.5 collective-permute-start.5
  87.6 8.7 %fusion.23 = f32[8,128]{1,0:T(8,128)S(1)} fusion(s32[3072]{0:T(1024)S(1)} %get-tuple-element.51, s32[3072]{0:T(1024)} %get-tuple-element.52, s32[128]{0:T(128)} %add_multiply_fusion, s32[8]{0:T(128)} %broadcast_multiply_fusion, pred[3072]{0:T(1024)(128)(4,1)S(1)} %fusion.124), kind=kLoop, calls=%fused_computation.29 | loop fusion | flops 66059264 | bytes 32288 | tf_op jit(solution)/shard_map/reduce_sum | solution.py:324
  96.3 0.7 add_bitcast_fusion
  97.7 16.8 %collective-permute-done.5 = bf16[1,384,1536]{1,2,0:T(8,128)(2,1)S(1)} collective-permute-done((bf16[1,384,1536]{1,2,0:T(8,128)(2,1)S(1)}, bf16[1,384,1536]{1,2,0:T(8,128)(2,1)S(1)}, u32[]{:S(2)}, u32[]{:S(2)}) %collective-permute-start.5) | collective-permute-done | bytes 1179680 | tf_op jit(solution)/shard_map/ppermute | solution.py:22
  114.8 2.8 copy.81
  117.7 14.5 %fusion.34 = f32[1024,768]{1,0:T(8,128)} fusion(bf16[1536,768]{0,1:T(8,128)(2,1)} %collective-permute-done.4, bf16[1536,768]{0,1:T(8,128)(2,1)} %bitcast.164, f32[1024]{0:T(1024)S(1)} %copy-done.15, s32[3072]{0:T(1024)S(1)} %get-tuple-element.51, s32[3072]{0:T(1024)S(1)} %copy-done.13, s32[1024]{0:T(1024)S(1)} %add_bitcast_fusion, ...), kind=kOutput, calls=%fused_computation.46 | convolution fusion | flops 4901044224 | bytes 7900160 | tf_op jit(solution)/shard_map/dot_general | solution.py:397
  132.2 9.1 %convolution_convert_fusion = bf16[1024,3072]{1,0:T(8,128)(2,1)S(1)} fusion(bf16[768,1536]{1,0:T(8,128)(2,1)S(1)} %collective-permute-done.6, bf16[768,1536]{1,0:T(8,128)(2,1)S(1)} %bitcast.161, pred[]{:T(512)S(6)} %eq.9, f32[1024,768]{1,0:T(8,128)} %fusion.34), kind=kOutput, calls=%fused_computation.41 | convolution fusion | flops 4863295488 | bytes 14155777 | tf_op jit(solution)/shard_map/dot_general | solution.py:400
  141.4 73.5 %shard_map.93 = f32[128,3072]{1,0:T(8,128)S(1)} custom-call(bf16[8,128,3072]{2,1,0:T(8,128)(2,1)S(1)} %bitcast.134), custom_call_target="tpu_custom_call" | custom-call | flops 6291456 | bytes 125829120 | tf_op jit(solution)/shard_map/pallas_call | solution.py:220
  214.9 3.0 fusion.77
  218.5 1.5 collective-permute-start.7
  220.6 12.9 %fusion.73 = bf16[3,2,128,1536]{3,2,0,1:T(8,128)(2,1)S(1)} fusion(bf16[1,3,3072,1536]{3,2,1,0:T(8,128)(2,1)} %param.10, bf16[1,128,3072]{2,1,0:T(8,128)(2,1)S(1)} %bitcast.174, bf16[1,128,3072]{2,1,0:T(8,128)(2,1)S(1)} %fusion.146), kind=kOutput, calls=%fused_computation.81 | convolution fusion | flops 7252082688 | bytes 32243712 | tf_op jit(solution)/shard_map/bsd,kdh->kbsh/dot_general | solution.py:336
  233.4 5.2 %collective-permute-done.7 = bf16[1,128,3072]{2,1,0:T(8,128)(2,1)} collective-permute-done((bf16[1,128,3072]{2,1,0:T(8,128)(2,1)S(1)}, bf16[1,128,3072]{2,1,0:T(8,128)(2,1)}, u32[]{:S(2)}, u32[]{:S(2)}) %collective-permute-start.7) | collective-permute-done | bytes 786464 | tf_op jit(solution)/shard_map/ppermute | solution.py:22
  238.6 9.1 %fusion.24 = bf16[1024,3072]{1,0:T(8,128)(2,1)} fusion(f32[1024]{0:T(1024)S(1)} %copy-done.15, s32[3072]{0:T(1024)S(1)} %get-tuple-element.51, s32[3072]{0:T(1024)S(1)} %copy-done.13, s32[1024]{0:T(1024)S(1)} %add_bitcast_fusion, pred[3072]{0:T(1024)(128)(4,1)S(1)} %copy-done.17), kind=kLoop, calls=%fused_computation.30 | loop fusion | flops 59768832 | bytes 6327296 | tf_op jit(solution)/shard_map/convert_element_type | solution.py:395
  248.2 1.2 copy.90
  249.8 1.3 copy.86
  251.0 1.2 copy.82
  252.2 13.5 %fusion.70 = bf16[3,2,128,1536]{3,2,0,1:T(8,128)(2,1)S(1)} fusion(bf16[1,3,3072,1536]{3,2,1,0:T(8,128)(2,1)} %param.10, bf16[1,128,3072]{2,1,0:T(8,128)(2,1)} %bitcast.28, bf16[1,128,3072]{2,1,0:T(8,128)(2,1)} %bitcast.27), kind=kOutput, calls=%fused_computation.80 | convolution fusion | flops 7252082688 | bytes 32243712 | tf_op jit(solution)/shard_map/bsd,kdh->kbsh/dot_general | solution.py:336
  266.2 1.2 copy.91
  267.8 1.2 copy.87
  269.4 2.6 fusion.33
  272.0 1.4 fusion.76
  273.4 0.8 slice-done.1
  274.5 1.4 fusion.41
  276.6 1.5 collective-permute-start.13
  278.1 1.4 fusion.38
  279.7 1.5 fusion.117
  281.1 0.6 collective-permute-start.12
  281.8 6.9 %collective-permute-done.13 = bf16[128,1536]{1,0:T(8,128)(2,1)S(1)} collective-permute-done((bf16[128,1536]{1,0:T(8,128)(2,1)S(1)}, bf16[128,1536]{1,0:T(8,128)(2,1)S(1)}, u32[]{:S(2)}, u32[]{:S(2)}) %collective-permute-start.13) | collective-permute-done | bytes 393248 | tf_op jit(solution)/shard_map/ppermute | solution.py:22
  288.7 1.4 fusion.31
  290.2 14.4 %collective-permute-done.12 = bf16[1,128,3072]{2,1,0:T(8,128)(2,1)S(1)} collective-permute-done((bf16[1,128,3072]{2,1,0:T(8,128)(2,1)S(1)}, bf16[1,128,3072]{2,1,0:T(8,128)(2,1)S(1)}, u32[]{:S(2)}, u32[]{:S(2)}) %collective-permute-start.12) | collective-permute-done | bytes 786464 | tf_op jit(solution)/shard_map/ppermute | solution.py:22
  304.6 1.2 fusion.118.own
  305.8 70.3 %shard_map.94 = bf16[8,128,3072]{2,1,0:T(8,128)(2,1)} custom-call(bf16[128,3072]{1,0:T(8,128)(2,1)} %fusion.118.own), custom_call_target="tpu_custom_call" | custom-call | bytes 125829120 | tf_op jit(solution)/shard_map/pallas_call | solution.py:304
  376.1 6.3 %multiply_convert_fusion.1 = bf16[768,1536]{1,0:T(8,128)(2,1)} fusion(bf16[1024,3072]{1,0:T(8,128)(2,1)} %bitcast.142, s32[]{:T(128)S(6)} %select_n.53, f32[1024,768]{1,0:T(8,128)S(1)} %copy-done.21), kind=kOutput, calls=%fused_computation.54 | convolution fusion | flops 2425356288 | bytes 8650756 | tf_op jit(solution)/shard_map/dot_general | solution.py:360
  382.4 2.9 convolution_multiply_fusion
  385.5 1.6 collective-permute-start.14
  387.1 11.8 %fusion.64 = bf16[1024,768]{1,0:T(8,128)(2,1)} fusion(f32[1024,768]{1,0:T(8,128)} %fusion.34, bf16[1024,3072]{1,0:T(8,128)(2,1)S(1)} %bitcast.144, bf16[768,1536]{1,0:T(8,128)(2,1)} %copy-done.20, bf16[768,1536]{1,0:T(8,128)(2,1)S(1)} %bitcast.162, pred[]{:T(512)S(6)} %eq.9), kind=kOutput, calls=%fused_computation.74 | convolution fusion | flops 4868014080 | bytes 15728641 | tf_op jit(solution)/shard_map/dot_general | solution.py:463
  399.0 2.2 add_convert_fusion.1
  401.2 4.0 multiply_convert_fusion
  405.7 3.3 copy.93
  409.0 1.3 slice.76
  410.7 7.4 %add_convert_fusion = bf16[1536,768]{0,1:T(8,128)(2,1)} fusion(bf16[1536,768]{0,1:T(8,128)(2,1)} %collective-permute-done.17, bf16[1024,768]{1,0:T(8,128)(2,1)} %fusion.64, bf16[1024,3072]{1,0:T(8,128)(2,1)} %fusion.24), kind=kOutput, calls=%fused_computation.51 | convolution fusion | flops 2420637696 | bytes 9437184 | tf_op jit(solution)/shard_map/dot_general | solution.py:360
  418.1 3.0 copy.95
  421.1 17.2 %collective-permute-done.16 = bf16[1,384,1536]{1,2,0:T(8,128)(2,1)S(1)} collective-permute-done((bf16[1,384,1536]{1,2,0:T(8,128)(2,1)}, bf16[1,384,1536]{1,2,0:T(8,128)(2,1)S(1)}, u32[]{:S(2)}, u32[]{:S(2)}) %collective-permute-start.16) | collective-permute-done | bytes 1179680 | tf_op jit(solution)/shard_map/ppermute | solution.py:22
  438.3 2.6 add_convert_fusion.2
  440.9 3.6 all-to-all-start.3
  445.2 26.5 %collective-permute-done.18 = bf16[1,1536,384]{2,1,0:T(8,128)(2,1)S(1)} collective-permute-done((bf16[1,1536,384]{2,1,0:T(8,128)(2,1)S(1)}, bf16[1,1536,384]{2,1,0:T(8,128)(2,1)S(1)}, u32[]{:S(2)}, u32[]{:S(2)}) %collective-permute-start.18) | collective-permute-done | bytes 1179680 | tf_op jit(solution)/shard_map/ppermute | solution.py:22
  471.7 1.3 add_convert_fusion.3
  473.0 5.6 %all-to-all-start.2 = ((bf16[8,192,384]{2,1,0:T(8,128)(2,1)}), bf16[8,192,384]{2,1,0:T(8,128)(2,1)S(1)}, u32[]{:S(2)}, u32[]{:S(2)}) async-start(bf16[8,192,384]{2,1,0:T(8,128)(2,1)} %bitcast.54), calls=%async_computation.2 | async-start | bytes 2359296 | tf_op jit(solution)/shard_map/all_to_all | solution.py:478
  478.7 1.2 copy.106
  479.9 25.7 %all-to-all-done.2 = bf16[8,192,384]{2,1,0:T(8,128)(2,1)S(1)} async-done(((bf16[8,192,384]{2,1,0:T(8,128)(2,1)}), bf16[8,192,384]{2,1,0:T(8,128)(2,1)S(1)}, u32[]{:S(2)}, u32[]{:S(2)}) %all-to-all-start.2) | async-done | bytes 1179680 | tf_op jit(solution)/shard_map/all_to_all | solution.py:478
  505.6 1.2 copy.105
  (110 shorter events, 11.7 us)
Async XLA Ops:
  0.6 37.5 %copy-start.7 = (bf16[3072,192]{0,1:T(8,128)(2,1)S(1)}, bf16[3072,192]{0,1:T(8,128)(2,1)}, u32[]{:S(2)}) copy-start(bf16[3072,192]{0,1:T(8,128)(2,1)} %param.9) | copy-start | bytes 3538948
  38.1 43.4 %copy-start.3 = (bf16[192,8,384]{2,0,1:T(8,128)(2,1)}, bf16[192,8,384]{2,0,1:T(8,128)(2,1)S(1)}, u32[]{:S(2)}) copy-start(bf16[192,8,384]{2,0,1:T(8,128)(2,1)S(1)} %all_to_all.67) | copy-start | bytes 3538948
  39.4 46.6 %all-to-all-start.1 = ((bf16[8,384,192]{1,2,0:T(8,128)(2,1)}), bf16[8,384,192]{1,2,0:T(8,128)(2,1)S(1)}, u32[]{:S(2)}, u32[]{:S(2)}) async-start(bf16[8,384,192]{1,2,0:T(8,128)(2,1)} %bitcast.129), calls=%async_computation.1 | async-start | bytes 2359296 | tf_op jit(solution)/shard_map/all_to_all | solution.py:373
  43.0 28.4 %collective-permute-start = (s32[1,1,1,1]{0,1,2,3:T(1,128)}, s32[1,1,1,1]{0,1,2,3:T(1,128)}, u32[]{:S(2)}, u32[]{:S(2)}) collective-permute-start(s32[1,1,1,1]{0,1,2,3:T(1,128)} %bitcast.2), channel_id=1, source_target_pairs={{0,8},{2,10},{4,12},{6,14},{8,0},{10,2},{12,4},{14,6},{1,9},{3,11}... | collective-permute-start | bytes 20 | tf_op jit(solution)/shard_map/ppermute | solution.py:22
  47.7 33.8 %collective-permute-start.3 = (bf16[1,1536,384]{2,1,0:T(8,128)(2,1)S(1)}, bf16[1,1536,384]{2,1,0:T(8,128)(2,1)}, u32[]{:S(2)}, u32[]{:S(2)}) collective-permute-start(bf16[1,1536,384]{2,1,0:T(8,128)(2,1)S(1)} %bitcast.150), channel_id=1, source_target_pairs={{0,1},{1,0},{2,3},{3,2},{4,5},{5,4},{6,7},{7,6},{8,9},{9,8},{10,11... | collective-permute-start | bytes 3538952 | tf_op jit(solution)/shard_map/ppermute | solution.py:22
  49.9 37.7 %copy-start.16 = (pred[3072]{0:T(1024)(128)(4,1)}, pred[3072]{0:T(1024)(128)(4,1)S(1)}, u32[]{:S(2)}) copy-start(pred[3072]{0:T(1024)(128)(4,1)S(1)} %fusion.124) | copy-start | bytes 9220
  72.0 3.6 collective-permute-start.1
  76.3 3.7 collective-permute-start.2
  86.1 31.6 %collective-permute-start.4 = (bf16[1536,768]{0,1:T(8,128)(2,1)}, bf16[1536,768]{0,1:T(8,128)(2,1)}, u32[]{:S(2)}, u32[]{:S(2)}) collective-permute-start(bf16[1536,768]{0,1:T(8,128)(2,1)} %bitcast.163), channel_id=1, source_target_pairs={{0,16},{16,0},{1,17},{17,1},{2,18},{18,2},{3,19},{19,3},{4,20},{20... | collective-permute-start | bytes 7077896 | tf_op jit(solution)/shard_map/ppermute | solution.py:22
  86.1 28.4 %collective-permute-start.5 = (bf16[1,384,1536]{1,2,0:T(8,128)(2,1)S(1)}, bf16[1,384,1536]{1,2,0:T(8,128)(2,1)S(1)}, u32[]{:S(2)}, u32[]{:S(2)}) collective-permute-start(bf16[1,384,1536]{1,2,0:T(8,128)(2,1)S(1)} %bitcast.148), channel_id=1, source_target_pairs={{0,1},{1,0},{2,3},{3,2},{4,5},{5,4},{6,7},{7,6},{8,9},{9,8},{10,11... | collective-permute-start | bytes 3538952 | tf_op jit(solution)/shard_map/ppermute | solution.py:22
  114.7 2.9 copy-start.13
  114.7 2.9 copy-start.15
  114.7 2.9 copy-start.17
  117.6 14.7 %copy-start.5 = (bf16[2,384,1536]{2,1,0:T(8,128)(2,1)S(1)}, bf16[2,384,1536]{2,1,0:T(8,128)(2,1)}, u32[]{:S(2)}) copy-start(bf16[2,384,1536]{2,1,0:T(8,128)(2,1)} %copy.81) | copy-start | bytes 7077892
  117.6 14.7 %collective-permute-start.6 = (bf16[768,1536]{1,0:T(8,128)(2,1)}, bf16[768,1536]{1,0:T(8,128)(2,1)S(1)}, u32[]{:S(2)}, u32[]{:S(2)}) collective-permute-start(bf16[768,1536]{1,0:T(8,128)(2,1)} %bitcast.160), channel_id=1, source_target_pairs={{0,16},{16,0},{1,17},{17,1},{2,18},{18,2},{3,19},{19,3},{4,20},{20... | collective-permute-start | bytes 7077896 | tf_op jit(solution)/shard_map/ppermute | solution.py:22
  132.2 9.1 %copy-start.20 = (bf16[768,1536]{1,0:T(8,128)(2,1)}, bf16[768,1536]{1,0:T(8,128)(2,1)S(1)}, u32[]{:S(2)}) copy-start(bf16[768,1536]{1,0:T(8,128)(2,1)S(1)} %collective-permute-done.6) | copy-start | bytes 7077892
  141.3 73.6 %copy-start.14 = (s32[3072]{0:T(1024)S(1)}, s32[3072]{0:T(1024)}, u32[]{:S(2)}) copy-start(s32[3072]{0:T(1024)} %iota_multiply_fusion) | copy-start | bytes 36868
  141.4 73.6 %copy-start.18 = (s32[128]{0:T(128)S(1)}, s32[128]{0:T(128)}, u32[]{:S(2)}) copy-start(s32[128]{0:T(128)} %get-tuple-element.49) | copy-start | bytes 1540
  141.4 73.6 %copy-start.19 = (s32[128]{0:T(128)S(1)}, s32[128]{0:T(128)}, u32[]{:S(2)}) copy-start(s32[128]{0:T(128)} %get-tuple-element.50) | copy-start | bytes 1540
  218.2 2.4 collective-permute-start.8
  218.5 20.1 %collective-permute-start.7 = (bf16[1,128,3072]{2,1,0:T(8,128)(2,1)S(1)}, bf16[1,128,3072]{2,1,0:T(8,128)(2,1)}, u32[]{:S(2)}, u32[]{:S(2)}) collective-permute-start(bf16[1,128,3072]{2,1,0:T(8,128)(2,1)S(1)} %fusion.146), channel_id=1, source_target_pairs={{0,1},{1,0},{2,3},{3,2},{4,5},{5,4},{6,7},{7,6},{8,9},{9,8},{10,11... | collective-permute-start | bytes 2359304 | tf_op jit(solution)/shard_map/ppermute | solution.py:22
  238.6 13.6 %collective-permute-start.9 = (bf16[128,3072]{1,0:T(8,128)(2,1)}, bf16[128,3072]{1,0:T(8,128)(2,1)}, u32[]{:S(2)}, u32[]{:S(2)}) collective-permute-start(bf16[128,3072]{1,0:T(8,128)(2,1)} %bitcast.19), channel_id=1, source_target_pairs={{0,16},{16,0},{1,17},{17,1},{2,18},{18,2},{3,19},{19,3},{4,20},{20... | collective-permute-start | bytes 2359304 | tf_op jit(solution)/shard_map/ppermute | solution.py:22
  267.4 1.9 copy-start.8
  267.8 1.6 copy-start.10
  269.4 2.6 copy-start.9
  269.4 4.1 slice-start
  272.0 2.3 slice-start.1
  272.0 2.5 slice-start.2
  274.5 2.1 copy-start.4
  275.9 3.7 collective-permute-start.11
  276.6 12.0 %collective-permute-start.13 = (bf16[128,1536]{1,0:T(8,128)(2,1)S(1)}, bf16[128,1536]{1,0:T(8,128)(2,1)S(1)}, u32[]{:S(2)}, u32[]{:S(2)}) collective-permute-start(bf16[128,1536]{1,0:T(8,128)(2,1)S(1)} %get-tuple-element.45), channel_id=1, source_target_pairs={{0,1},{1,0},{2,3},{3,2},{4,5},{5,4},{6,7},{7,6},{8,9},{9,8},{10,11... | collective-permute-start | bytes 1179656 | tf_op jit(solution)/shard_map/ppermute | solution.py:22
  279.6 10.6 %collective-permute-start.10 = (bf16[128,3072]{1,0:T(8,128)(2,1)S(1)}, bf16[128,3072]{1,0:T(8,128)(2,1)S(1)}, u32[]{:S(2)}, u32[]{:S(2)}) collective-permute-start(bf16[128,3072]{1,0:T(8,128)(2,1)S(1)} %fusion.38), channel_id=1, source_target_pairs={{0,16},{16,0},{1,17},{17,1},{2,18},{18,2},{3,19},{19,3},{4,20},{20... | collective-permute-start | bytes 2359304 | tf_op jit(solution)/shard_map/ppermute | solution.py:22
  281.1 23.5 %collective-permute-start.12 = (bf16[1,128,3072]{2,1,0:T(8,128)(2,1)S(1)}, bf16[1,128,3072]{2,1,0:T(8,128)(2,1)S(1)}, u32[]{:S(2)}, u32[]{:S(2)}) collective-permute-start(bf16[1,128,3072]{2,1,0:T(8,128)(2,1)S(1)} %fusion.117), channel_id=1, source_target_pairs={{0,1},{1,0},{2,3},{3,2},{4,5},{5,4},{6,7},{7,6},{8,9},{9,8},{10,11... | collective-permute-start | bytes 2359304 | tf_op jit(solution)/shard_map/ppermute | solution.py:22
  288.7 1.4 copy-start.12
  305.8 70.3 %copy-start.21 = (f32[1024,768]{1,0:T(8,128)S(1)}, f32[1024,768]{1,0:T(8,128)}, u32[]{:S(2)}) copy-start(f32[1024,768]{1,0:T(8,128)} %fusion.34) | copy-start | bytes 9437188
  376.1 6.3 %copy-start.2 = (bf16[8,128,3072]{2,1,0:T(8,128)(2,1)S(1)}, bf16[8,128,3072]{2,1,0:T(8,128)(2,1)}, u32[]{:S(2)}) copy-start(bf16[8,128,3072]{2,1,0:T(8,128)(2,1)} %shard_map.94) | copy-start | bytes 18874372
  382.4 3.0 copy-start.1
  382.4 4.7 copy-start.6
  382.4 18.8 %slice-start.3 = ((s8[6291456]{0:T(1024)(128)(4,1)}), s8[4194304]{0:T(1024)(128)(4,1)S(1)}, s32[]{:S(2)}) async-start(s8[6291456]{0:T(1024)(128)(4,1)} %bitcast.140), calls=%async_computation.7 | async-start | bytes 8388608
  385.5 15.7 %slice-start.4 = ((s8[6291456]{0:T(1024)(128)(4,1)}), s8[2097152]{0:T(1024)(128)(4,1)S(1)}, s32[]{:S(2)}) async-start(s8[6291456]{0:T(1024)(128)(4,1)} %bitcast.140), calls=%async_computation.8 | async-start | bytes 4194304
  385.5 13.4 %collective-permute-start.14 = (bf16[128,1536]{1,0:T(8,128)(2,1)S(1)}, bf16[128,1536]{1,0:T(8,128)(2,1)S(1)}, u32[]{:S(2)}, u32[]{:S(2)}) collective-permute-start(bf16[128,1536]{1,0:T(8,128)(2,1)S(1)} %get-tuple-element.43), channel_id=1, source_target_pairs={{0,1},{1,0},{2,3},{3,2},{4,5},{5,4},{6,7},{7,6},{8,9},{9,8},{10,11... | collective-permute-start | bytes 1179656 | tf_op jit(solution)/shard_map/ppermute | solution.py:22
  387.1 11.9 %collective-permute-start.15 = (bf16[768,1536]{1,0:T(8,128)(2,1)}, bf16[768,1536]{1,0:T(8,128)(2,1)S(1)}, u32[]{:S(2)}, u32[]{:S(2)}) collective-permute-start(bf16[768,1536]{1,0:T(8,128)(2,1)} %multiply_convert_fusion.1), channel_id=1, source_target_pairs={{0,16},{16,0},{1,17},{17,1},{2,18},{18,2},{3,19},{19,3},{4,20},{20... | collective-permute-start | bytes 7077896 | tf_op jit(solution)/shard_map/ppermute | solution.py:22
  398.9 2.2 copy-start.11
  398.9 2.2 copy-start.22
  405.2 5.6 %collective-permute-start.17 = (bf16[1536,768]{0,1:T(8,128)(2,1)}, bf16[1536,768]{0,1:T(8,128)(2,1)}, u32[]{:S(2)}, u32[]{:S(2)}) collective-permute-start(bf16[1536,768]{0,1:T(8,128)(2,1)} %multiply_convert_fusion), channel_id=1, source_target_pairs={{0,16},{16,0},{1,17},{17,1},{2,18},{18,2},{3,19},{19,3},{4,20},{20... | collective-permute-start | bytes 7077896 | tf_op jit(solution)/shard_map/ppermute | solution.py:22
  408.9 9.1 %copy-start = (bf16[2,384,1536]{1,2,0:T(8,128)(2,1)}, bf16[2,384,1536]{1,2,0:T(8,128)(2,1)S(1)}, u32[]{:S(2)}) copy-start(bf16[2,384,1536]{1,2,0:T(8,128)(2,1)S(1)} %copy.93) | copy-start | bytes 7077892
  410.2 28.1 %collective-permute-start.16 = (bf16[1,384,1536]{1,2,0:T(8,128)(2,1)}, bf16[1,384,1536]{1,2,0:T(8,128)(2,1)S(1)}, u32[]{:S(2)}, u32[]{:S(2)}) collective-permute-start(bf16[1,384,1536]{1,2,0:T(8,128)(2,1)} %slice.76), channel_id=1, source_target_pairs={{0,1},{1,0},{2,3},{3,2},{4,5},{5,4},{6,7},{7,6},{8,9},{9,8},{10,11... | collective-permute-start | bytes 3538952 | tf_op jit(solution)/shard_map/ppermute | solution.py:22
  440.9 32.1 %all-to-all-start.3 = ((bf16[384,8,192]{0,2,1:T(8,128)(2,1)}), bf16[384,8,192]{0,2,1:T(8,128)(2,1)S(1)}, u32[]{:S(2)}, u32[]{:S(2)}) async-start(bf16[384,8,192]{0,2,1:T(8,128)(2,1)} %bitcast.56), calls=%async_computation.3 | async-start | bytes 2359296 | tf_op jit(solution)/shard_map/all_to_all | solution.py:476
  444.6 27.1 %collective-permute-start.18 = (bf16[1,1536,384]{2,1,0:T(8,128)(2,1)S(1)}, bf16[1,1536,384]{2,1,0:T(8,128)(2,1)S(1)}, u32[]{:S(2)}, u32[]{:S(2)}) collective-permute-start(bf16[1,1536,384]{2,1,0:T(8,128)(2,1)S(1)} %slice.67), channel_id=1, source_target_pairs={{0,1},{1,0},{2,3},{3,2},{4,5},{5,4},{6,7},{7,6},{8,9},{9,8},{10,11... | collective-permute-start | bytes 3538952 | tf_op jit(solution)/shard_map/ppermute | solution.py:22
  473.0 32.6 %all-to-all-start.2 = ((bf16[8,192,384]{2,1,0:T(8,128)(2,1)}), bf16[8,192,384]{2,1,0:T(8,128)(2,1)S(1)}, u32[]{:S(2)}, u32[]{:S(2)}) async-start(bf16[8,192,384]{2,1,0:T(8,128)(2,1)} %bitcast.54), calls=%async_computation.2 | async-start | bytes 2359296 | tf_op jit(solution)/shard_map/all_to_all | solution.py:478

commit v4 on v3

--- a/solution.py
+++ b/solution.py
@@ -368,23 +368,8 @@
     length = SEQ // n_mp
     half = D // 2
 
-    up = lax.all_to_all(gen_up, "dp", split_axis=1, concat_axis=0, tiled=True)
-    gen_down, up = lax.optimization_barrier((gen_down, up))
-    down = lax.all_to_all(gen_down, "dp", split_axis=0, concat_axis=1, tiled=True)
-    share = up.shape[1]
-    up = xor_gather(up, "mp", mp_bits).reshape(n_mp, half, share)
-    up = up.transpose(1, 0, 2).reshape(half, n_mp * share)
-    up = jnp.concatenate([up, swap(up, "group", 1)], axis=0)
-    down = xor_gather(down, "mp", mp_bits).reshape(n_mp * share, half)
-    down_other = swap(down, "group", 1)
-    down = jnp.where(
-        group == 0,
-        jnp.concatenate([down, down_other], axis=1),
-        jnp.concatenate([down_other, down], axis=1),
-    )
-
-    seeds = xor_gather(noise_seeds, "dp", bits_of("dp")[::-1])
-    seeds = seeds.transpose(tuple(range(seeds.ndim))[::-1]).reshape(1, n_dp)
+    seeds = [noise_seeds] + [swap(noise_seeds, "dp", mask) for mask in range(1, n_dp)]
+    seeds = jnp.concatenate(seeds)[None]
     index = lax.broadcasted_iota(jnp.int32, (n_dp, n_dp), 0)
     column = lax.broadcasted_iota(jnp.int32, (n_dp, n_dp), 1)
     seeds = jnp.sum(jnp.where(index ^ lax.axis_index("dp") == column, seeds, 0), axis=1)
@@ -394,6 +379,22 @@
     feature = (lax.broadcasted_iota(jnp.int32, shape, 2) + group * half) % D
     normed = rms_norm(hashed(seeds, 0, tokens, feature)).astype(jnp.bfloat16)
     normed = normed.reshape(n_dp * length, D)
+    up = lax.all_to_all(gen_up, "dp", split_axis=1, concat_axis=0, tiled=True)
+    gen_down, up, normed = lax.optimization_barrier((gen_down, up, normed))
+    down = lax.all_to_all(gen_down, "dp", split_axis=0, concat_axis=1, tiled=True)
+    share = up.shape[1]
+    up, down = lax.optimization_barrier((xor_gather(up, "mp", mp_bits), down))
+    up = up.reshape(n_mp, half, share)
+    up = up.transpose(1, 0, 2).reshape(half, n_mp * share)
+    up = jnp.concatenate([up, swap(up, "group", 1)], axis=0)
+    down = xor_gather(down, "mp", mp_bits).reshape(n_mp * share, half)
+    down_other = swap(down, "group", 1)
+    down = jnp.where(
+        group == 0,
+        jnp.concatenate([down, down_other], axis=1),
+        jnp.concatenate([down_other, down], axis=1),
+    )
+
     before = jnp.dot(normed, up, preferred_element_type=jnp.float32)
     hidden = jax.nn.gelu(before, approximate=True).astype(jnp.bfloat16)
 
@@ -443,7 +444,6 @@
     gap = gap.reshape(length, D).astype(jnp.bfloat16)
     gap, latents = lax.optimization_barrier((gap, latents))
     gap_all = gather_over_dp(gap).reshape(n_dp * length, D)
-    score_gap = tokens_to_features(gap, "mp")
 
     def over_batch(value):
         return value / batch_size
@@ -459,12 +459,12 @@
     gap_all, down_kept = lax.optimization_barrier((gap_all, down_kept))
     grad_down = (down_kept + down_sent.astype(jnp.float32)).astype(jnp.bfloat16)
     grad_down = grad_down.reshape((2,) * len(mp_bits) + (share, half))
+    gap_all, grad_down = lax.optimization_barrier((gap_all, grad_down))
 
     slope = lax.dot_general(
         gap_all, down, (((1,), (1,)), ((), ())), preferred_element_type=jnp.float32
     )
     change = (slope * gelu_slope(before)).astype(jnp.bfloat16)
-    change, score_gap, grad_down = lax.optimization_barrier((change, score_gap, grad_down))
     up_sent = over_batch(contract_first(normed[:, half:], change)).astype(jnp.bfloat16)
     up_sent = swap(up_sent, "group", 1)
     up_kept = over_batch(contract_first(normed[:, :half], change))
@@ -475,6 +475,8 @@
     grad_down = grad_down.astype(jnp.bfloat16)
     grad_down = lax.all_to_all(grad_down, "dp", split_axis=1, concat_axis=0, tiled=True)
     grad_up = xor_scatter(grad_up, "mp", mp_bits).astype(jnp.bfloat16)
+    grad_up, gap = lax.optimization_barrier((grad_up, gap))
+    score_gap = tokens_to_features(gap, "mp")
     grad_up = lax.all_to_all(grad_up, "dp", split_axis=0, concat_axis=1, tiled=True)
     return (latents[None], score_gap[None], grad_up, grad_down)
 

time: 512 us -> 515 us (level)
  blocking collectives: 36 us -> 0 us
  starting transfers between devices: 27.7 us -> 49.4 us
  waiting for transfers between devices: 139 us -> 156 us
  local copies, waits for them, and re-layouts: 28 us -> 36.5 us
  other arithmetic: 37.1 us -> 31.8 us
    all_to_all x1 -> x0, blocking collectives: 36 us -> none  [per_device(): up = lax.all_to_all(gen_up, 'dp', split_axis=1, concat_axis=0, tiled=True)]
    ppermute x19 -> x23, waiting for transfers between devices: 114 us -> 139 us  [swap(): lax.ppermute(shard, axis, [(i, i ^ bit) for i in range(lax.axis_size(axis...]
    ppermute x19 -> x23, starting transfers between devices: 14.9 us -> 27 us  [swap(): lax.ppermute(shard, axis, [(i, i ^ bit) for i in range(lax.axis_size(axis...]
    all_to_all x1, waiting for transfers between devices: 25.7 us -> 15.3 us  [per_device(): lax.all_to_all(grad_up, 'dp', split_axis=0, concat_axis=1, tiled=True)]
  transfers between devices with their start and end apart: 22 -> 27, of which waited for: 11 -> 13; matrix products, arithmetic and copies ran while one was open for 19% -> 18% of each run, Pallas kernels for 0% -> 0%
where the time goes in v4:
time: 515 us; the launch traced here: 510 us
  waiting for transfers between devices  156 us (30%)
  Pallas kernels  145 us (28%)
  matrix products  88.1 us (17%)
  starting transfers between devices  49.4 us (10%)
  local copies, waits for them, and re-layouts  36.5 us (7%)
  other arithmetic  31.8 us (6%)
    ppermute x23, waiting for transfers between devices, swap(): lax.ppermute(shard, axis, [(i, i ^ bit) for i in range(lax.axis_size(axis...  139 us
    pallas_call x1, Pallas kernels, sum_over_dp(): pl.pallas_call(functools.partial(sum_kernel, line), out_shape=jax.ShapeDt...  75.1 us
    pallas_call x1, Pallas kernels, gather_over_dp(): pl.pallas_call(functools.partial(gather_kernel, line), out_shape=jax.Shap...  70 us
    dot_general x2, matrix products, project(): jnp.einsum('bsd,kdh->kbsh', normed, weights_in, preferred_element_type=jn...  28.1 us
    ppermute x23, starting transfers between devices, swap(): lax.ppermute(shard, axis, [(i, i ^ bit) for i in range(lax.axis_size(axis...  27 us
    dot_general x4, matrix products, contract_first(): lax.dot_general(left, right, (((0,), (0,)), ((), ())), preferred_element_...  24.4 us
    all_to_all x1, waiting for transfers between devices, per_device(): lax.all_to_all(grad_up, 'dp', split_axis=0, concat_axis=1, tiled=True)  15.3 us
    reduce_sum x2, other arithmetic, rms_norm(): jnp.mean(value * value, axis=-1, keepdims=True) + NORM_EPS  11 us
  transfers between devices with their start and end apart: 27, of which 13 were waited for; matrix products, arithmetic and copies ran while one was open for 18% of the time, Pallas kernels for 0%

profile of v4, /device:TPU:0, one launch (start us, length us, event | category | flops | bytes accessed | tf_op | source)
XLA Modules:
  0.0 510.0 jit_solution(4187737398614606940)
XLA Ops:
  0.6 3.0 collective-permute-start
  3.6 1.6 collective-permute-start.1
  5.2 3.0 collective-permute-start.3
  8.2 1.3 collective-permute-start.4
  9.5 2.4 copy.110
  11.9 4.9 all-to-all-start
  17.5 3.9 collective-permute-start.5
  21.4 1.5 collective-permute-start.6
  22.9 16.0 %collective-permute-done.5 = s32[1]{0:T(128)} collective-permute-done((s32[1]{0:T(128)}, s32[1]{0:T(128)}, u32[]{:S(2)}, u32[]{:S(2)}) %collective-permute-start.5) | collective-permute-done | bytes 36 | tf_op jit(solution)/shard_map/ppermute | solution.py:22
  39.6 4.4 concatenate.43
  44.2 7.9 %fusion.23 = f32[8,128]{1,0:T(8,128)S(1)} fusion(s32[3072]{0:T(1024)S(1)} %get-tuple-element.57, s32[3072]{0:T(1024)S(1)} %get-tuple-element.58, s32[128]{0:T(128)S(1)} %get-tuple-element.55, s32[8]{0:T(128)S(1)} %broadcast_multiply_fusion, pred[3072]{0:T(1024)(128)(4,1)S(1)} %fusion.125), kind=kLoop, calls=%fused_computation.29 | loop fusion | flops 66059264 | bytes 32288 | tf_op jit(solution)/shard_map/reduce_sum | solution.py:324
  52.2 9.1 %fusion.24 = bf16[1024,3072]{1,0:T(8,128)(2,1)} fusion(f32[1024]{0:T(1024)S(1)} %multiply_bitcast_fusion, s32[3072]{0:T(1024)S(1)} %get-tuple-element.57, s32[3072]{0:T(1024)S(1)} %get-tuple-element.58, s32[1024]{0:T(1024)S(1)} %add_bitcast_fusion, pred[3072]{0:T(1024)(128)(4,1)S(1)} %fusion.125), kind=kLoop, calls=%fused_computation.30 | loop fusion | flops 59768832 | bytes 6327296 | tf_op jit(solution)/shard_map/convert_element_type | solution.py:380
  62.5 7.7 %all-to-all-start.1 = ((bf16[8,384,192]{1,2,0:T(8,128)(2,1)}), bf16[8,384,192]{1,2,0:T(8,128)(2,1)}, u32[]{:S(2)}, u32[]{:S(2)}) async-start(bf16[8,384,192]{1,2,0:T(8,128)(2,1)} %bitcast.132), calls=%async_computation.1 | async-start | bytes 2359296 | tf_op jit(solution)/shard_map/all_to_all | solution.py:384
  70.2 1.6 collective-permute-start.7
  71.8 25.4 %collective-permute-done.7 = bf16[1,1536,384]{2,1,0:T(8,128)(2,1)S(1)} collective-permute-done((bf16[1,1536,384]{2,1,0:T(8,128)(2,1)S(1)}, bf16[1,1536,384]{2,1,0:T(8,128)(2,1)S(1)}, u32[]{:S(2)}, u32[]{:S(2)}) %collective-permute-start.7) | collective-permute-done | bytes 1179680 | tf_op jit(solution)/shard_map/ppermute | solution.py:22
  97.4 1.7 all-to-all-done.1
  99.2 1.5 collective-permute-start.9
  100.7 2.6 copy.80
  103.3 22.8 %collective-permute-done.9 = bf16[1,384,1536]{1,2,0:T(8,128)(2,1)S(1)} collective-permute-done((bf16[1,384,1536]{1,2,0:T(8,128)(2,1)}, bf16[1,384,1536]{1,2,0:T(8,128)(2,1)S(1)}, u32[]{:S(2)}, u32[]{:S(2)}) %collective-permute-start.9) | collective-permute-done | bytes 1179680 | tf_op jit(solution)/shard_map/ppermute | solution.py:22
  126.1 1.5 pad_maximum_fusion.1
  127.6 2.6 copy.81
  131.0 9.9 %fusion.34 = f32[1024,768]{1,0:T(8,128)} fusion(bf16[1024,3072]{1,0:T(8,128)(2,1)} %fusion.24, bf16[1536,768]{0,1:T(8,128)(2,1)} %collective-permute-done.8, bf16[1536,768]{0,1:T(8,128)(2,1)} %bitcast.164), kind=kOutput, calls=%fused_computation.46 | convolution fusion | flops 4841275392 | bytes 14155776 | tf_op jit(solution)/shard_map/dot_general | solution.py:398
  140.9 8.7 %convolution_convert_fusion = bf16[1024,3072]{1,0:T(8,128)(2,1)S(1)} fusion(bf16[768,1536]{1,0:T(8,128)(2,1)S(1)} %collective-permute-done.10, bf16[768,1536]{1,0:T(8,128)(2,1)S(1)} %bitcast.161, pred[]{:T(512)S(6)} %eq.9, f32[1024,768]{1,0:T(8,128)} %fusion.34), kind=kOutput, calls=%fused_computation.41 | convolution fusion | flops 4863295488 | bytes 14155777 | tf_op jit(solution)/shard_map/dot_general | solution.py:401
  149.6 75.1 %shard_map.93 = f32[128,3072]{1,0:T(8,128)S(1)} custom-call(bf16[8,128,3072]{2,1,0:T(8,128)(2,1)S(1)} %bitcast.134), custom_call_target="tpu_custom_call" | custom-call | flops 6291456 | bytes 125829120 | tf_op jit(solution)/shard_map/pallas_call | solution.py:220
  224.7 3.0 fusion.77
  228.3 1.6 collective-permute-start.11
  230.3 14.3 %fusion.73 = bf16[3,2,128,1536]{3,2,0,1:T(8,128)(2,1)} fusion(bf16[1,3,3072,1536]{3,2,1,0:T(8,128)(2,1)} %param.10, bf16[1,128,3072]{2,1,0:T(8,128)(2,1)S(1)} %bitcast.173, bf16[1,128,3072]{2,1,0:T(8,128)(2,1)S(1)} %fusion.147), kind=kOutput, calls=%fused_computation.81 | convolution fusion | flops 7252082688 | bytes 32243712 | tf_op jit(solution)/shard_map/bsd,kdh->kbsh/dot_general | solution.py:336
  244.6 3.7 collective-permute-done.11
  248.4 1.8 fusion.141
  253.2 1.2 copy.82
  254.5 13.8 %fusion.70 = bf16[3,2,128,1536]{3,2,0,1:T(8,128)(2,1)S(1)} fusion(bf16[1,3,3072,1536]{3,2,1,0:T(8,128)(2,1)} %param.10, bf16[1,128,3072]{2,1,0:T(8,128)(2,1)} %bitcast.26, bf16[1,128,3072]{2,1,0:T(8,128)(2,1)} %bitcast.25), kind=kOutput, calls=%fused_computation.80 | convolution fusion | flops 7252082688 | bytes 32243712 | tf_op jit(solution)/shard_map/bsd,kdh->kbsh/dot_general | solution.py:336
  272.0 2.6 fusion.33
  274.6 1.4 fusion.76
  277.1 1.4 fusion.41
  279.2 1.6 collective-permute-start.17
  280.8 1.4 fusion.38
  282.3 1.5 fusion.118
  284.3 6.9 %collective-permute-done.17 = bf16[128,1536]{1,0:T(8,128)(2,1)S(1)} collective-permute-done((bf16[128,1536]{1,0:T(8,128)(2,1)S(1)}, bf16[128,1536]{1,0:T(8,128)(2,1)S(1)}, u32[]{:S(2)}, u32[]{:S(2)}) %collective-permute-start.17) | collective-permute-done | bytes 393248 | tf_op jit(solution)/shard_map/ppermute | solution.py:22
  291.3 1.4 fusion.31
  292.7 14.4 %collective-permute-done.16 = bf16[1,128,3072]{2,1,0:T(8,128)(2,1)S(1)} collective-permute-done((bf16[1,128,3072]{2,1,0:T(8,128)(2,1)S(1)}, bf16[1,128,3072]{2,1,0:T(8,128)(2,1)S(1)}, u32[]{:S(2)}, u32[]{:S(2)}) %collective-permute-start.16) | collective-permute-done | bytes 786464 | tf_op jit(solution)/shard_map/ppermute | solution.py:22
  307.2 1.2 fusion.119.own
  308.3 70.0 %shard_map.94 = bf16[8,128,3072]{2,1,0:T(8,128)(2,1)} custom-call(bf16[128,3072]{1,0:T(8,128)(2,1)} %fusion.119.own), custom_call_target="tpu_custom_call" | custom-call | bytes 125829120 | tf_op jit(solution)/shard_map/pallas_call | solution.py:304
  378.3 7.2 %multiply_convert_fusion.1 = bf16[768,1536]{1,0:T(8,128)(2,1)} fusion(bf16[1024,3072]{1,0:T(8,128)(2,1)} %bitcast.143, s32[]{:T(128)S(6)} %select_n.53, f32[1024,768]{1,0:T(8,128)} %fusion.34), kind=kOutput, calls=%fused_computation.54 | convolution fusion | flops 2425356288 | bytes 8650756 | tf_op jit(solution)/shard_map/dot_general | solution.py:360
  385.6 5.8 %convolution_multiply_fusion = f32[768,1536]{1,0:T(8,128)S(1)} fusion(bf16[1024,3072]{1,0:T(8,128)(2,1)} %bitcast.144, s32[]{:T(128)S(6)} %select_n.54, f32[1024,768]{1,0:T(8,128)} %fusion.34), kind=kOutput, calls=%fused_computation.55 | convolution fusion | flops 2424176640 | bytes 11010052 | tf_op jit(solution)/shard_map/dot_general | solution.py:360
  391.4 4.1 add_convert_fusion.1
  396.3 7.3 %fusion.64 = bf16[1024,768]{1,0:T(8,128)(2,1)S(1)} fusion(f32[1024,768]{1,0:T(8,128)S(1)} %copy-done.13, bf16[1024,3072]{1,0:T(8,128)(2,1)S(1)} %bitcast.147, bf16[768,1536]{1,0:T(8,128)(2,1)S(1)} %copy-done.12, bf16[768,1536]{1,0:T(8,128)(2,1)S(1)} %bitcast.162, pred[]{:T(512)S(6)} %eq.9), kind=kOutput, calls=%fused_computation.74 | convolution fusion | flops 4868014080 | bytes 15728641 | tf_op jit(solution)/shard_map/dot_general | solution.py:464
  403.6 4.0 multiply_convert_fusion
  408.1 3.0 copy.93
  411.1 1.2 slice.76
  412.4 1.5 collective-permute-start.19
  413.9 7.3 %add_convert_fusion = bf16[1536,768]{0,1:T(8,128)(2,1)} fusion(bf16[1536,768]{0,1:T(8,128)(2,1)} %collective-permute-done.20, bf16[1024,768]{1,0:T(8,128)(2,1)} %copy-done.14, bf16[1024,3072]{1,0:T(8,128)(2,1)} %fusion.24), kind=kOutput, calls=%fused_computation.51 | convolution fusion | flops 2420637696 | bytes 9437184 | tf_op jit(solution)/shard_map/dot_general | solution.py:360
  421.2 3.0 copy.95
  424.2 16.2 %collective-permute-done.19 = bf16[1,384,1536]{1,2,0:T(8,128)(2,1)S(1)} collective-permute-done((bf16[1,384,1536]{1,2,0:T(8,128)(2,1)}, bf16[1,384,1536]{1,2,0:T(8,128)(2,1)S(1)}, u32[]{:S(2)}, u32[]{:S(2)}) %collective-permute-start.19) | collective-permute-done | bytes 1179680 | tf_op jit(solution)/shard_map/ppermute | solution.py:22
  440.4 2.6 add_convert_fusion.2
  443.0 4.3 all-to-all-start.3
  447.4 1.6 collective-permute-start.21
  449.0 25.5 %collective-permute-done.21 = bf16[1,1536,384]{2,1,0:T(8,128)(2,1)S(1)} collective-permute-done((bf16[1,1536,384]{2,1,0:T(8,128)(2,1)S(1)}, bf16[1,1536,384]{2,1,0:T(8,128)(2,1)S(1)}, u32[]{:S(2)}, u32[]{:S(2)}) %collective-permute-start.21) | collective-permute-done | bytes 1179680 | tf_op jit(solution)/shard_map/ppermute | solution.py:22
  474.5 1.3 fusion.116
  475.9 5.6 %all-to-all-start.2 = ((bf16[8,192,384]{2,1,0:T(8,128)(2,1)}), bf16[8,192,384]{2,1,0:T(8,128)(2,1)S(1)}, u32[]{:S(2)}, u32[]{:S(2)}) async-start(bf16[8,192,384]{2,1,0:T(8,128)(2,1)} %bitcast.148), calls=%async_computation.2 | async-start | bytes 2359296 | tf_op jit(solution)/shard_map/all_to_all | solution.py:480
  481.6 1.6 collective-permute-start.22
  483.2 7.2 %collective-permute-done.22 = bf16[128,1536]{1,0:T(8,128)(2,1)S(1)} collective-permute-done((bf16[128,1536]{1,0:T(8,128)(2,1)S(1)}, bf16[128,1536]{1,0:T(8,128)(2,1)S(1)}, u32[]{:S(2)}, u32[]{:S(2)}) %collective-permute-start.22) | collective-permute-done | bytes 393248 | tf_op jit(solution)/shard_map/ppermute | solution.py:22
  490.5 2.8 copy.106
  493.2 15.3 %all-to-all-done.2 = bf16[8,192,384]{2,1,0:T(8,128)(2,1)S(1)} async-done(((bf16[8,192,384]{2,1,0:T(8,128)(2,1)}), bf16[8,192,384]{2,1,0:T(8,128)(2,1)S(1)}, u32[]{:S(2)}, u32[]{:S(2)}) %all-to-all-start.2) | async-done | bytes 1179680 | tf_op jit(solution)/shard_map/all_to_all | solution.py:480
  508.5 1.2 copy.105
  (106 shorter events, 14.2 us)
Async XLA Ops:
  0.6 16.9 %collective-permute-start = (s32[1]{0:T(128)}, s32[1]{0:T(128)}, u32[]{:S(2)}, u32[]{:S(2)}) collective-permute-start(s32[1]{0:T(128)} %param.6), channel_id=1, source_target_pairs={{0,2},{2,0},{4,6},{6,4},{8,10},{10,8},{12,14},{14,12},{1,3},{3,1},... | collective-permute-start | bytes 20 | tf_op jit(solution)/shard_map/ppermute | solution.py:22
  3.6 17.8 %collective-permute-start.1 = (s32[1]{0:T(128)}, s32[1]{0:T(128)}, u32[]{:S(2)}, u32[]{:S(2)}) collective-permute-start(s32[1]{0:T(128)} %param.6), channel_id=1, source_target_pairs={{0,4},{2,6},{4,0},{6,2},{8,12},{10,14},{12,8},{14,10},{1,5},{3,7},... | collective-permute-start | bytes 20 | tf_op jit(solution)/shard_map/ppermute | solution.py:22
  5.2 17.7 %collective-permute-start.2 = (s32[1]{0:T(128)}, s32[1]{0:T(128)}, u32[]{:S(2)}, u32[]{:S(2)}) collective-permute-start(s32[1]{0:T(128)} %param.6), channel_id=1, source_target_pairs={{0,6},{2,4},{4,2},{6,0},{8,14},{10,12},{12,10},{14,8},{1,7},{3,5},... | collective-permute-start | bytes 20 | tf_op jit(solution)/shard_map/ppermute | solution.py:22
  5.2 17.7 %collective-permute-start.3 = (s32[1]{0:T(128)}, s32[1]{0:T(128)}, u32[]{:S(2)}, u32[]{:S(2)}) collective-permute-start(s32[1]{0:T(128)} %param.6), channel_id=1, source_target_pairs={{0,8},{2,10},{4,12},{6,14},{8,0},{10,2},{12,4},{14,6},{1,9},{3,11}... | collective-permute-start | bytes 20 | tf_op jit(solution)/shard_map/ppermute | solution.py:22
  8.2 14.7 %collective-permute-start.4 = (s32[1]{0:T(128)}, s32[1]{0:T(128)}, u32[]{:S(2)}, u32[]{:S(2)}) collective-permute-start(s32[1]{0:T(128)} %param.6), channel_id=1, source_target_pairs={{0,10},{2,8},{4,14},{6,12},{8,2},{10,0},{12,6},{14,4},{1,11},{3,9}... | collective-permute-start | bytes 20 | tf_op jit(solution)/shard_map/ppermute | solution.py:22
  11.9 49.4 %all-to-all-start = ((bf16[192,8,384]{2,0,1:T(8,128)(2,1)}), bf16[192,8,384]{2,0,1:T(8,128)(2,1)S(1)}, u32[]{:S(2)}, u32[]{:S(2)}) async-start(bf16[192,8,384]{2,0,1:T(8,128)(2,1)} %bitcast.133), calls=%async_computation | async-start | bytes 2359296 | tf_op jit(solution)/shard_map/all_to_all | solution.py:382
  17.5 21.3 %collective-permute-start.5 = (s32[1]{0:T(128)}, s32[1]{0:T(128)}, u32[]{:S(2)}, u32[]{:S(2)}) collective-permute-start(s32[1]{0:T(128)} %param.6), channel_id=1, source_target_pairs={{0,12},{2,14},{4,8},{6,10},{8,4},{10,6},{12,0},{14,2},{1,13},{3,15... | collective-permute-start | bytes 20 | tf_op jit(solution)/shard_map/ppermute | solution.py:22
  21.4 18.2 %collective-permute-start.6 = (s32[1]{0:T(128)}, s32[1]{0:T(128)}, u32[]{:S(2)}, u32[]{:S(2)}) collective-permute-start(s32[1]{0:T(128)} %param.6), channel_id=1, source_target_pairs={{0,14},{2,12},{4,10},{6,8},{8,6},{10,4},{12,2},{14,0},{1,15},{3,13... | collective-permute-start | bytes 20 | tf_op jit(solution)/shard_map/ppermute | solution.py:22
  52.2 9.1 %copy-start.5 = (bf16[3072,192]{0,1:T(8,128)(2,1)S(1)}, bf16[3072,192]{0,1:T(8,128)(2,1)}, u32[]{:S(2)}) copy-start(bf16[3072,192]{0,1:T(8,128)(2,1)} %param.9) | copy-start | bytes 3538948
  62.5 36.7 %all-to-all-start.1 = ((bf16[8,384,192]{1,2,0:T(8,128)(2,1)}), bf16[8,384,192]{1,2,0:T(8,128)(2,1)}, u32[]{:S(2)}, u32[]{:S(2)}) async-start(bf16[8,384,192]{1,2,0:T(8,128)(2,1)} %bitcast.132), calls=%async_computation.1 | async-start | bytes 2359296 | tf_op jit(solution)/shard_map/all_to_all | solution.py:384
  70.2 27.0 %collective-permute-start.7 = (bf16[1,1536,384]{2,1,0:T(8,128)(2,1)S(1)}, bf16[1,1536,384]{2,1,0:T(8,128)(2,1)S(1)}, u32[]{:S(2)}, u32[]{:S(2)}) collective-permute-start(bf16[1,1536,384]{2,1,0:T(8,128)(2,1)S(1)} %bitcast.150), channel_id=1, source_target_pairs={{0,1},{1,0},{2,3},{3,2},{4,5},{5,4},{6,7},{7,6},{8,9},{9,8},{10,11... | collective-permute-start | bytes 3538952 | tf_op jit(solution)/shard_map/ppermute | solution.py:22
  99.2 26.9 %collective-permute-start.9 = (bf16[1,384,1536]{1,2,0:T(8,128)(2,1)}, bf16[1,384,1536]{1,2,0:T(8,128)(2,1)S(1)}, u32[]{:S(2)}, u32[]{:S(2)}) collective-permute-start(bf16[1,384,1536]{1,2,0:T(8,128)(2,1)} %bitcast.11), channel_id=1, source_target_pairs={{0,1},{1,0},{2,3},{3,2},{4,5},{5,4},{6,7},{7,6},{8,9},{9,8},{10,11... | collective-permute-start | bytes 3538952 | tf_op jit(solution)/shard_map/ppermute | solution.py:22
  103.3 27.6 %collective-permute-start.8 = (bf16[1536,768]{0,1:T(8,128)(2,1)}, bf16[1536,768]{0,1:T(8,128)(2,1)}, u32[]{:S(2)}, u32[]{:S(2)}) collective-permute-start(bf16[1536,768]{0,1:T(8,128)(2,1)} %bitcast.163), channel_id=1, source_target_pairs={{0,16},{16,0},{1,17},{17,1},{2,18},{18,2},{3,19},{19,3},{4,20},{20... | collective-permute-start | bytes 7077896 | tf_op jit(solution)/shard_map/ppermute | solution.py:22
  130.3 10.7 %collective-permute-start.10 = (bf16[768,1536]{1,0:T(8,128)(2,1)}, bf16[768,1536]{1,0:T(8,128)(2,1)S(1)}, u32[]{:S(2)}, u32[]{:S(2)}) collective-permute-start(bf16[768,1536]{1,0:T(8,128)(2,1)} %bitcast.160), channel_id=1, source_target_pairs={{0,16},{16,0},{1,17},{17,1},{2,18},{18,2},{3,19},{19,3},{4,20},{20... | collective-permute-start | bytes 7077896 | tf_op jit(solution)/shard_map/ppermute | solution.py:22
  131.0 10.0 %copy-start.3 = (bf16[2,384,1536]{2,1,0:T(8,128)(2,1)S(1)}, bf16[2,384,1536]{2,1,0:T(8,128)(2,1)}, u32[]{:S(2)}) copy-start(bf16[2,384,1536]{2,1,0:T(8,128)(2,1)} %copy.81) | copy-start | bytes 7077892
  140.9 8.7 %copy-start.11 = (bf16[768,1536]{1,0:T(8,128)(2,1)}, bf16[768,1536]{1,0:T(8,128)(2,1)S(1)}, u32[]{:S(2)}) copy-start(bf16[768,1536]{1,0:T(8,128)(2,1)S(1)} %collective-permute-done.10) | copy-start | bytes 7077892
  228.0 2.4 collective-permute-start.12
  228.3 20.1 %collective-permute-start.11 = (bf16[1,128,3072]{2,1,0:T(8,128)(2,1)S(1)}, bf16[1,128,3072]{2,1,0:T(8,128)(2,1)}, u32[]{:S(2)}, u32[]{:S(2)}) collective-permute-start(bf16[1,128,3072]{2,1,0:T(8,128)(2,1)S(1)} %fusion.147), channel_id=1, source_target_pairs={{0,1},{1,0},{2,3},{3,2},{4,5},{5,4},{6,7},{7,6},{8,9},{9,8},{10,11... | collective-permute-start | bytes 2359304 | tf_op jit(solution)/shard_map/ppermute | solution.py:22
  248.4 6.1 %collective-permute-start.13 = (bf16[128,3072]{1,0:T(8,128)(2,1)}, bf16[128,3072]{1,0:T(8,128)(2,1)}, u32[]{:S(2)}, u32[]{:S(2)}) collective-permute-start(bf16[128,3072]{1,0:T(8,128)(2,1)} %bitcast.17), channel_id=1, source_target_pairs={{0,16},{16,0},{1,17},{17,1},{2,18},{18,2},{3,19},{19,3},{4,20},{20... | collective-permute-start | bytes 2359304 | tf_op jit(solution)/shard_map/ppermute | solution.py:22
  270.0 1.9 copy-start.6
  270.4 1.6 copy-start.8
  271.9 2.6 copy-start.7
  271.9 4.1 slice-start
  274.6 2.3 slice-start.1
  274.6 2.5 slice-start.2
  277.1 2.1 copy-start.2
  278.5 3.8 collective-permute-start.15
  279.2 12.0 %collective-permute-start.17 = (bf16[128,1536]{1,0:T(8,128)(2,1)S(1)}, bf16[128,1536]{1,0:T(8,128)(2,1)S(1)}, u32[]{:S(2)}, u32[]{:S(2)}) collective-permute-start(bf16[128,1536]{1,0:T(8,128)(2,1)S(1)} %get-tuple-element.51), channel_id=1, source_target_pairs={{0,1},{1,0},{2,3},{3,2},{4,5},{5,4},{6,7},{7,6},{8,9},{9,8},{10,11... | collective-permute-start | bytes 1179656 | tf_op jit(solution)/shard_map/ppermute | solution.py:22
  282.2 10.5 %collective-permute-start.14 = (bf16[128,3072]{1,0:T(8,128)(2,1)S(1)}, bf16[128,3072]{1,0:T(8,128)(2,1)S(1)}, u32[]{:S(2)}, u32[]{:S(2)}) collective-permute-start(bf16[128,3072]{1,0:T(8,128)(2,1)S(1)} %fusion.38), channel_id=1, source_target_pairs={{0,16},{16,0},{1,17},{17,1},{2,18},{18,2},{3,19},{19,3},{4,20},{20... | collective-permute-start | bytes 2359304 | tf_op jit(solution)/shard_map/ppermute | solution.py:22
  283.8 23.3 %collective-permute-start.16 = (bf16[1,128,3072]{2,1,0:T(8,128)(2,1)S(1)}, bf16[1,128,3072]{2,1,0:T(8,128)(2,1)S(1)}, u32[]{:S(2)}, u32[]{:S(2)}) collective-permute-start(bf16[1,128,3072]{2,1,0:T(8,128)(2,1)S(1)} %fusion.118), channel_id=1, source_target_pairs={{0,1},{1,0},{2,3},{3,2},{4,5},{5,4},{6,7},{7,6},{8,9},{9,8},{10,11... | collective-permute-start | bytes 2359304 | tf_op jit(solution)/shard_map/ppermute | solution.py:22
  291.3 1.4 copy-start.10
  378.3 17.2 %slice-start.5 = ((s8[6291456]{0:T(1024)(128)(4,1)}), s8[2097152]{0:T(1024)(128)(4,1)S(1)}, s32[]{:S(2)}) async-start(s8[6291456]{0:T(1024)(128)(4,1)} %bitcast.145), calls=%async_computation.9 | async-start | bytes 4194304
  385.5 5.9 %collective-permute-start.18 = (bf16[768,1536]{1,0:T(8,128)(2,1)}, bf16[768,1536]{1,0:T(8,128)(2,1)}, u32[]{:S(2)}, u32[]{:S(2)}) collective-permute-start(bf16[768,1536]{1,0:T(8,128)(2,1)} %multiply_convert_fusion.1), channel_id=1, source_target_pairs={{0,16},{16,0},{1,17},{17,1},{2,18},{18,2},{3,19},{19,3},{4,20},{20... | collective-permute-start | bytes 7077896 | tf_op jit(solution)/shard_map/ppermute | solution.py:22
  385.6 10.0 %slice-start.6 = ((s8[6291456]{0:T(1024)(128)(4,1)}), s8[4194304]{0:T(1024)(128)(4,1)S(1)}, s32[]{:S(2)}) async-start(s8[6291456]{0:T(1024)(128)(4,1)} %bitcast.145), calls=%async_computation.10 | async-start | bytes 8388608
  391.4 4.1 copy-start.4
  391.4 4.1 copy-start.12
  391.4 4.9 copy-start.13
  391.4 12.1 %slice-start.3 = ((s8[6291456]{0:T(1024)(128)(4,1)}), s8[4194304]{0:T(1024)(128)(4,1)S(1)}, s32[]{:S(2)}) async-start(s8[6291456]{0:T(1024)(128)(4,1)} %bitcast.141), calls=%async_computation.7 | async-start | bytes 8388608
  396.3 7.3 %slice-start.4 = ((s8[6291456]{0:T(1024)(128)(4,1)}), s8[2097152]{0:T(1024)(128)(4,1)S(1)}, s32[]{:S(2)}) async-start(s8[6291456]{0:T(1024)(128)(4,1)} %bitcast.141), calls=%async_computation.8 | async-start | bytes 4194304
  403.6 4.0 copy-start.14
  407.6 6.3 %collective-permute-start.20 = (bf16[1536,768]{0,1:T(8,128)(2,1)}, bf16[1536,768]{0,1:T(8,128)(2,1)}, u32[]{:S(2)}, u32[]{:S(2)}) collective-permute-start(bf16[1536,768]{0,1:T(8,128)(2,1)} %multiply_convert_fusion), channel_id=1, source_target_pairs={{0,16},{16,0},{1,17},{17,1},{2,18},{18,2},{3,19},{19,3},{4,20},{20... | collective-permute-start | bytes 7077896 | tf_op jit(solution)/shard_map/ppermute | solution.py:22
  411.1 10.1 %copy-start = (bf16[2,384,1536]{1,2,0:T(8,128)(2,1)}, bf16[2,384,1536]{1,2,0:T(8,128)(2,1)S(1)}, u32[]{:S(2)}) copy-start(bf16[2,384,1536]{1,2,0:T(8,128)(2,1)S(1)} %copy.93) | copy-start | bytes 7077892
  412.4 28.1 %collective-permute-start.19 = (bf16[1,384,1536]{1,2,0:T(8,128)(2,1)}, bf16[1,384,1536]{1,2,0:T(8,128)(2,1)S(1)}, u32[]{:S(2)}, u32[]{:S(2)}) collective-permute-start(bf16[1,384,1536]{1,2,0:T(8,128)(2,1)} %slice.76), channel_id=1, source_target_pairs={{0,1},{1,0},{2,3},{3,2},{4,5},{5,4},{6,7},{7,6},{8,9},{9,8},{10,11... | collective-permute-start | bytes 3538952 | tf_op jit(solution)/shard_map/ppermute | solution.py:22
  443.0 32.8 %all-to-all-start.3 = ((bf16[384,8,192]{0,2,1:T(8,128)(2,1)}), bf16[384,8,192]{0,2,1:T(8,128)(2,1)}, u32[]{:S(2)}, u32[]{:S(2)}) async-start(bf16[384,8,192]{0,2,1:T(8,128)(2,1)} %bitcast.56), calls=%async_computation.3 | async-start | bytes 2359296 | tf_op jit(solution)/shard_map/all_to_all | solution.py:476
  447.4 34.1 %copy-start.1 = (bf16[128,3072]{1,0:T(8,128)(2,1)S(1)}, bf16[128,3072]{1,0:T(8,128)(2,1)}, u32[]{:S(2)}) copy-start(bf16[128,3072]{1,0:T(8,128)(2,1)} %fusion.119.own) | copy-start | bytes 2359300
  447.4 27.1 %collective-permute-start.21 = (bf16[1,1536,384]{2,1,0:T(8,128)(2,1)S(1)}, bf16[1,1536,384]{2,1,0:T(8,128)(2,1)S(1)}, u32[]{:S(2)}, u32[]{:S(2)}) collective-permute-start(bf16[1,1536,384]{2,1,0:T(8,128)(2,1)S(1)} %slice.67), channel_id=1, source_target_pairs={{0,1},{1,0},{2,3},{3,2},{4,5},{5,4},{6,7},{7,6},{8,9},{9,8},{10,11... | collective-permute-start | bytes 3538952 | tf_op jit(solution)/shard_map/ppermute | solution.py:22
  475.9 32.6 %all-to-all-start.2 = ((bf16[8,192,384]{2,1,0:T(8,128)(2,1)}), bf16[8,192,384]{2,1,0:T(8,128)(2,1)S(1)}, u32[]{:S(2)}, u32[]{:S(2)}) async-start(bf16[8,192,384]{2,1,0:T(8,128)(2,1)} %bitcast.148), calls=%async_computation.2 | async-start | bytes 2359296 | tf_op jit(solution)/shard_map/all_to_all | solution.py:480
  481.6 8.9 %collective-permute-start.22 = (bf16[128,1536]{1,0:T(8,128)(2,1)S(1)}, bf16[128,1536]{1,0:T(8,128)(2,1)S(1)}, u32[]{:S(2)}, u32[]{:S(2)}) collective-permute-start(bf16[128,1536]{1,0:T(8,128)(2,1)S(1)} %constant_dynamic-slice_fusion.1), channel_id=1, source_target_pairs={{0,1},{1,0},{2,3},{3,2},{4,5},{5,4},{6,7},{7,6},{8,9},{9,8},{10,11... | collective-permute-start | bytes 1179656 | tf_op jit(solution)/shard_map/ppermute | solution.py:22
  490.5 19.3 %copy-start.9 = (bf16[1,256,1536]{2,1,0:T(8,128)(2,1)}, bf16[1,256,1536]{2,1,0:T(8,128)(2,1)S(1)}, u32[]{:S(2)}) copy-start(bf16[1,256,1536]{2,1,0:T(8,128)(2,1)S(1)} %bitcast_dynamic-update-slice_fusion) | copy-start | bytes 2359300
